TPU v7x, 512 devices: a whole 4x8x8 slice. The times are simulated.
512 devices in a mesh: seq: 16 (over z, core), batch: 16 (over y_lo, x), tp: 2 (over y_hi).
Axes of the slice: x: 4, y: 8 (y_hi: 2, y_lo: 4; y = y_hi * 4 + y_lo), z: 8, core: 2. Of those that a mesh axis runs over, the one named last changes fastest.
Arguments:
- pre_q: bfloat16 [16, 2048, 4096], P('batch', 'seq', 'tp'), may hold values from -40 to 40
- pre_k: bfloat16 [16, 2048, 512], P('batch', 'seq', 'tp'), may hold values from -40 to 40
- pre_v: bfloat16 [16, 2048, 512], P('batch', 'seq', 'tp'), may hold values from -12 to 12
- owner_map: int32 [16, 128, 1], P('batch', 'seq'), may hold values from 0 to 15; in each aligned block of 8 rows (0 to 7, 8 to 15, ..., all dimensions but the last counted through in order) at most 2 rows name the same one
- cache_k: bfloat16 [128, 256, 512], P('batch', 'seq', 'tp'), may hold values from -6 to 6
- cache_v: bfloat16 [128, 256, 512], P('batch', 'seq', 'tp'), may hold values from -12 to 12
- tables: int32 [32, 64], P('batch', 'seq'), may hold values from 0 to 7, as said below
- lengths: int32 [32], P('batch'), may hold values from 1 to 1024, 16384 in all
- dec_q: float32 [32, 3, 4096], P('batch', None, 'tp'), may hold values from -40 to 40
- dec_k: float32 [32, 3, 512], P('batch', None, 'tp'), may hold values from -40 to 40
- dec_v: float32 [32, 3, 512], P('batch', None, 'tp'), may hold values from -12 to 12
- w_out: bfloat16 [4096, 8192], P('tp', 'seq'), may hold values from -0.09375 to 0.09375
Outputs:
- pre_out: bfloat16 [16, 2048, 4096], P('batch', 'seq', 'tp')
- dec_out: float32 [32, 3, 8192], P('batch', None, 'seq')
Inputs may be any that keep to these rules, and one draw needn't show every extreme that they name: `owner_map`: in each aligned block of 8 rows (the pages of one index of seq of one span) no owner is named more than 2 times. `tables`: within one owner's 2 requests and one index of seq, the 8 entries are distinct.
All inputs are finite; a program needn't handle non-finite values. No bound on the sum of `lengths` on one device may be relied on, other than what follows from the above.
Results may differ from a plain program's by a relative error of at most 0.0033.
Values may be sent and summed in bfloat16 or wider, within the bound.
No kernel may reach another device: no remote copies, remote signals or barrier semaphores. Data moves between devices by JAX's collectives and lax.ppermute only.
A program may use at most 64 MiB of HBM per device.

v0:
```python
import jax
import jax.numpy as jnp
from jax import lax
from jax.sharding import PartitionSpec as P

HD = 128


highest = lax.Precision.HIGHEST
floor_score = -1e30


def merged(value, axis, combine):
    everything = jax.tree.map(lambda part: lax.all_gather(part, axis), value)
    leading = jax.tree.map(lambda part: part[0], everything)

    def step(k, so_far):
        return combine(so_far, jax.tree.map(lambda part: part[k], everything))

    return lax.fori_loop(1, lax.axis_size(axis), step, leading)


def block_math(query_block, key_rows, value_rows, start_row):
    block_rows = query_block.shape[0]
    key_count = key_rows.shape[0]
    scaling = HD ** (-0.5)
    scores = (
        jnp.einsum("qagd,kad->agqk", query_block, key_rows, preferred_element_type=jnp.float32)
        * scaling
    )
    query_pos = start_row + jnp.arange(block_rows)
    visible = jnp.arange(key_count)[None, :] <= query_pos[:, None]
    masked = jnp.where(visible, scores, floor_score)
    row_peak = jnp.max(masked, axis=-1, keepdims=True)
    weights = jnp.where(visible, jnp.exp(scores - row_peak), 0.0)
    row_total = jnp.sum(weights, axis=-1)
    mixture = jnp.einsum(
        "agqk,kad->qagd",
        weights.astype(jnp.bfloat16),
        value_rows,
        preferred_element_type=jnp.float32,
    )
    return (mixture / jnp.transpose(row_total, (2, 0, 1))[..., None]).astype(jnp.bfloat16)


def attend_whole(queries, key_rows, value_rows):
    row_count = queries.shape[0]
    block_rows = min(512, row_count)
    pieces = []
    for block_id in range(row_count // block_rows):
        end_row = (block_id + 1) * block_rows
        pieces.append(
            block_math(
                queries[block_id * block_rows : end_row],
                key_rows[:end_row],
                value_rows[:end_row],
                block_id * block_rows,
            )
        )
    return jnp.concatenate(pieces, axis=0)


def partial_state(scores, visible, value_rows, pattern):
    masked = jnp.where(visible, scores, floor_score)
    row_peak = jnp.max(masked, axis=-1)
    weights = jnp.where(visible, jnp.exp(scores - row_peak[..., None]), 0.0)
    return (
        row_peak,
        jnp.sum(weights, axis=-1),
        jnp.einsum(pattern, weights, value_rows, precision=highest),
    )


def combine(first_state, second_state):
    row_peak = jnp.maximum(first_state[0], second_state[0])
    first_scale = jnp.exp(first_state[0] - row_peak)
    second_scale = jnp.exp(second_state[0] - row_peak)
    return (
        row_peak,
        first_state[1] * first_scale + second_state[1] * second_scale,
        first_state[2] * first_scale[..., None] + second_state[2] * second_scale[..., None],
    )


def shared_state(dec_queries, key_rows, value_rows, kept_rows):
    scores = jnp.einsum("rnkgd,tkd->rnkgt", dec_queries, key_rows, precision=highest) * HD ** (-0.5)
    return partial_state(scores, kept_rows, value_rows, "rnkgt,tkd->rnkgd")


def local(
    pre_q, pre_k, pre_v, owner_map, cache_k, cache_v, tables, lengths, dec_q, dec_k, dec_v, w_out
):
    seq_count = lax.axis_size("seq")
    seq_index = lax.axis_index("seq")
    bat_index = lax.axis_index("batch")
    tok_rows = pre_q.shape[1]
    q_heads = pre_q.shape[2] // HD
    k_heads = pre_k.shape[2] // HD
    group_size = q_heads // k_heads
    span_rows = tok_rows * seq_count
    queries = pre_q[0]
    key_rows = pre_k[0]
    value_rows = pre_v[0]
    per_device = q_heads // seq_count
    wide_q = queries.reshape(tok_rows, seq_count, per_device, HD)
    wide_k = jnp.repeat(key_rows.reshape(tok_rows, k_heads, HD), group_size, axis=1).reshape(
        tok_rows, seq_count, per_device, HD
    )
    wide_v = jnp.repeat(value_rows.reshape(tok_rows, k_heads, HD), group_size, axis=1).reshape(
        tok_rows, seq_count, per_device, HD
    )
    head_q = lax.all_to_all(wide_q, "seq", split_axis=1, concat_axis=0, tiled=True)
    head_k = lax.all_to_all(wide_k, "seq", split_axis=1, concat_axis=0, tiled=True)
    head_v = lax.all_to_all(wide_v, "seq", split_axis=1, concat_axis=0, tiled=True)
    head_count = head_q.shape[2]
    result = attend_whole(
        head_q, head_k.reshape(span_rows, head_count, HD), head_v.reshape(span_rows, head_count, HD)
    )
    prefill_rows = lax.all_to_all(result, "seq", split_axis=0, concat_axis=1, tiled=True).reshape(
        tok_rows, q_heads * HD
    )
    requests = dec_q.shape[0]
    new_count = dec_q.shape[1]
    dec_queries = dec_q.reshape(requests, new_count, k_heads, group_size, HD)
    table_count = tables.shape[1]
    page_rows = cache_k.shape[1]
    cached_k = (
        cache_k[tables].astype(jnp.float32).reshape(requests, table_count * page_rows, k_heads, HD)
    )
    cached_v = (
        cache_v[tables].astype(jnp.float32).reshape(requests, table_count * page_rows, k_heads, HD)
    )
    positions = (
        (jnp.arange(table_count)[:, None] * seq_count + seq_index) * page_rows
        + jnp.arange(page_rows)[None, :]
    ).reshape(-1)
    live_rows = (positions[None, :] < lengths[:, None])[:, None, None, None, :]
    scores = jnp.einsum("rnkgd,rtkd->rnkgt", dec_queries, cached_k, precision=highest) * HD ** (
        -0.5
    )
    partial_value = partial_state(scores, live_rows, cached_v, "rnkgt,rtkd->rnkgd")
    page_count = tok_rows // page_rows
    own_k = key_rows.reshape(page_count, page_rows, k_heads * HD)
    own_v = value_rows.reshape(page_count, page_rows, k_heads * HD)
    owners = owner_map[0, :, 0]
    piece_k = lax.all_gather(own_k, "batch", axis=0, tiled=True)
    piece_v = lax.all_gather(own_v, "batch", axis=0, tiled=True)
    piece_owner = lax.all_gather(owners.astype(jnp.bfloat16), "batch", axis=0, tiled=True)
    piece_pages = piece_k.shape[0]
    kept_rows = jnp.repeat(
        piece_owner.astype(jnp.float32) == bat_index.astype(jnp.float32), page_rows
    )
    fresh = shared_state(
        dec_queries,
        piece_k.astype(jnp.float32).reshape(piece_pages * page_rows, k_heads, HD),
        piece_v.astype(jnp.float32).reshape(piece_pages * page_rows, k_heads, HD),
        kept_rows,
    )
    partial_value = combine(partial_value, fresh)
    partial_value = merged(partial_value, "seq", combine)
    new_k = dec_k.reshape(requests, new_count, k_heads, HD)
    new_v = dec_v.reshape(requests, new_count, k_heads, HD)
    scores = jnp.einsum("rnkgd,rjkd->rnkgj", dec_queries, new_k, precision=highest) * HD ** (-0.5)
    causal = (jnp.arange(new_count)[None, :] <= jnp.arange(new_count)[:, None])[
        None, :, None, None, :
    ]
    partial_value = combine(
        partial_value, partial_state(scores, causal, new_v, "rnkgj,rjkd->rnkgd")
    )
    attention = (partial_value[2] / partial_value[1][..., None]).reshape(
        requests * new_count, q_heads * HD
    )
    projected = jnp.dot(attention, w_out.astype(jnp.float32), precision=highest)
    dec_out = lax.psum(projected, "tp").reshape(requests, new_count, projected.shape[1])
    return (prefill_rows[None], dec_out)


def solution(mesh):
    placed = (
        P("batch", "seq", "tp"),
        P("batch", "seq", "tp"),
        P("batch", "seq", "tp"),
        P("batch", "seq", None),
        P("batch", "seq", "tp"),
        P("batch", "seq", "tp"),
        P("batch", "seq"),
        P("batch"),
        P("batch", None, "tp"),
        P("batch", None, "tp"),
        P("batch", None, "tp"),
        P("tp", "seq"),
    )
    return jax.shard_map(
        local,
        mesh=mesh,
        in_specs=placed,
        out_specs=(P("batch", "seq", "tp"), P("batch", None, "seq")),
        check_vma=False,
    )
```

profile of v0, /device:TPU:1, one launch (start us, length us, event | category | flops | bytes accessed | tf_op | source)
XLA Modules:
  0.0 235.9 jit_solution(12094448383075277757)
XLA Ops:
  7.3 0.7 all-gather.5.cloned.1.call-update
  8.0 0.9 reshape_squeeze.17
  8.9 0.9 broadcast_in_dim.139
  9.8 11.8 %all-to-all-start.2 = ((bf16[128,16,1,128]{3,0,2,1:T(8,128)(2,1)}), bf16[128,16,1,128]{3,0,2,1:T(8,128)(2,1)S(1)}, u32[]{:S(2)}, u32[]{:S(2)}) async-start(bf16[128,16,1,128]{3,0,2,1:T(8,128)(2,1)} %bitcast.16), calls=%async_computation.2 | async-start | bytes 1048576 | tf_op jit(solution)/shard_map/all_to_all | solution.py:114
  21.6 0.9 reshape_squeeze.15
  22.5 16.7 %all-to-all-done.2 = bf16[128,16,1,128]{3,0,2,1:T(8,128)(2,1)S(1)} async-done(((bf16[128,16,1,128]{3,0,2,1:T(8,128)(2,1)}), bf16[128,16,1,128]{3,0,2,1:T(8,128)(2,1)S(1)}, u32[]{:S(2)}, u32[]{:S(2)}) %all-to-all-start.2) | async-done | bytes 524320 | tf_op jit(solution)/shard_map/all_to_all | solution.py:114
  39.1 0.9 broadcast_in_dim.136
  40.0 3.5 %all-to-all-start = ((bf16[128,16,1,128]{3,0,2,1:T(8,128)(2,1)}), bf16[128,16,1,128]{3,0,2,1:T(8,128)(2,1)S(1)}, u32[]{:S(2)}, u32[]{:S(2)}) async-start(bf16[128,16,1,128]{3,0,2,1:T(8,128)(2,1)} %bitcast.279), calls=%async_computation | async-start | bytes 1048576 | tf_op jit(solution)/shard_map/all_to_all | solution.py:113
  43.6 0.7 all-gather.7.cloned.1.call-update
  44.3 2.1 copy.152
  46.3 1.3 dynamic-slice
  48.5 36.8 %all-reduce = bf16[128]{0:T(256)(128)(2,1)S(1)} all-reduce(bf16[128]{0:T(256)(128)(2,1)S(1)} %dynamic-update-slice), channel_id=2, replica_groups=mesh['seq'=16,'batch'=16,'tp'=2] {'batch'}, use_global_device_ids=true, to_apply=%add | all-reduce | flops 128 | bytes 512
  85.5 0.7 reshape.426
  86.2 13.2 %all-to-all-start.1 = ((bf16[128,16,1,128]{0,3,2,1:T(8,128)(2,1)}), bf16[128,16,1,128]{0,3,2,1:T(8,128)(2,1)}, u32[]{:S(2)}, u32[]{:S(2)}) async-start(bf16[128,16,1,128]{0,3,2,1:T(8,128)(2,1)} %bitcast.278), calls=%async_computation.1 | async-start | bytes 1048576 | tf_op jit(solution)/shard_map/all_to_all | solution.py:112
  99.5 0.7 add.158
  102.7 0.8 slice.75
  103.5 0.8 slice.73
  104.2 0.7 slice.70
  105.0 0.7 slice.69
  106.3 10.6 %all-to-all-done.1 = bf16[128,16,1,128]{0,3,2,1:T(8,128)(2,1)} async-done(((bf16[128,16,1,128]{0,3,2,1:T(8,128)(2,1)}), bf16[128,16,1,128]{0,3,2,1:T(8,128)(2,1)}, u32[]{:S(2)}, u32[]{:S(2)}) %all-to-all-start.1) | async-done | bytes 524320 | tf_op jit(solution)/shard_map/all_to_all | solution.py:112
  116.8 2.0 copy.154
  118.9 1.1 fusion.112
  120.0 0.8 fusion.3
  120.8 1.1 fusion.7
  121.9 1.5 fusion.50
  124.0 0.8 fusion.10
  124.8 1.0 fusion.59
  126.9 0.8 fusion.39
  129.1 1.0 reduce.8
  130.2 0.9 reshape.478
  131.1 4.3 %all-to-all-start.3 = ((bf16[16,2,8192]{2,1,0:T(2,128)(2,1)}), bf16[16,2,8192]{2,1,0:T(2,128)(2,1)}, u32[]{:S(2)}, u32[]{:S(2)}) async-start(bf16[16,2,8192]{2,1,0:T(2,128)(2,1)} %reshape.478), calls=%async_computation.3 | async-start | bytes 1048576 | tf_op jit(solution)/shard_map/all_to_all | solution.py:119
  136.7 14.3 %all-to-all-done.3 = bf16[16,2,8192]{2,1,0:T(2,128)(2,1)} async-done(((bf16[16,2,8192]{2,1,0:T(2,128)(2,1)}), bf16[16,2,8192]{2,1,0:T(2,128)(2,1)}, u32[]{:S(2)}, u32[]{:S(2)}) %all-to-all-start.3) | async-done | bytes 524320 | tf_op jit(solution)/shard_map/all_to_all | solution.py:119
  151.0 2.2 reshape.479
  153.3 0.9 copy.200
  154.1 1.3 copy.157
  155.4 1.0 copy.180
  156.5 1.4 reshape.427
  157.8 1.3 select_reduce_fusion.2
  159.1 1.1 fusion.111
  160.3 14.7 %all_gather.25 = f32[16,2,3,2,8]{4,3,2,1,0:T(2,128)S(1)} all-gather(f32[1,2,3,2,8]{4,3,2,1,0:T(2,128)S(1)} %get-tuple-element.244), channel_id=1, replica_groups=mesh['seq'=16,'batch'=16,'tp'=2] {'seq'}, dimensions={0}, use_global_device_ids=true | all-gather | bytes 6528 | tf_op jit(solution)/shard_map/all_gather | solution.py:14
  175.0 15.2 %all_gather.26 = f32[16,2,3,2,8]{4,3,2,1,0:T(2,128)S(1)} all-gather(f32[1,2,3,2,8]{4,3,2,1,0:T(2,128)S(1)} %get-tuple-element.243), channel_id=1, replica_groups=mesh['seq'=16,'batch'=16,'tp'=2] {'seq'}, dimensions={0}, use_global_device_ids=true | all-gather | bytes 6528 | tf_op jit(solution)/shard_map/all_gather | solution.py:14
  190.3 1.5 fusion.35
  191.8 1.4 reshape.429
  193.2 1.8 fusion.34
  195.0 17.9 %all-gather.1 = f32[32,3,2,8,128]{4,3,2,1,0:T(8,128)S(1)} all-gather(f32[2,3,2,8,128]{4,3,2,1,0:T(8,128)S(1)} %copy.171), channel_id=3, replica_groups=mesh['seq'=16,'batch'=16,'tp'=2] {'seq'}, dimensions={0}, use_global_device_ids=true | all-gather | bytes 835584 | tf_op jit(solution)/shard_map/all_gather | solution.py:14
  212.9 2.4 %while.19 = (s32[]{:T(128)}, f32[2,3,2,8]{3,2,1,0:T(2,128)S(1)}, f32[2,3,2,8]{3,2,1,0:T(2,128)S(1)}, f32[2,3,2,8,128]{4,3,2,1,0:T(8,128)S(1)}, f32[16,2,3,2,8]{4...) while((s32[]{:T(128)}, f32[2,3,2,8]{3,2,1,0:T(2,128)S(1)}, ...), condition=%wide.region_13.14_spmd, body=%wide.region_12.13_spmd.sunk | while | flops 37445 | bytes 151447 | solution.py:20
  215.8 0.9 fusion.113
  216.7 11.7 %psum.7 = f32[2,3,512]{2,1,0:T(4,128)S(1)} all-reduce(f32[2,3,512]{2,1,0:T(4,128)S(1)} %reshape.433), channel_id=1, replica_groups=mesh['seq'=16,'batch'=16,'tp'=2] {'tp'}, use_global_device_ids=true, to_apply=%region_16.17 | all-reduce | flops 3072 | bytes 24576 | tf_op jit(solution)/shard_map/psum | solution.py:174
  (127 shorter events, 11.2 us)
Async XLA Ops:
  7.2 208.6 %copy-start = (bf16[2048,512]{1,0:T(8,128)(2,1)S(1)}, bf16[2048,512]{1,0:T(8,128)(2,1)}, u32[]{:S(2)}) copy-start(bf16[2048,512]{1,0:T(8,128)(2,1)} %param.25) | copy-start | bytes 6291460
  7.2 41.1 %copy-start.19 = (s32[1,8,1]{1,2,0:T(1,128)S(1)}, s32[1,8,1]{1,2,0:T(1,128)}, u32[]{:S(2)}) copy-start(s32[1,8,1]{1,2,0:T(1,128)} %param.17) | copy-start | bytes 100
  7.2 79.0 %copy-start.9 = (f32[2,3,2048]{2,0,1:T(2,128)S(1)}, f32[2,3,2048]{2,0,1:T(2,128)}, u32[]{:S(2)}) copy-start(f32[2,3,2048]{2,0,1:T(2,128)} %param.22) | copy-start | bytes 147460
  7.2 93.0 %copy-start.17 = (s32[2,4]{1,0:T(2,128)S(1)}, s32[2,4]{1,0:T(2,128)}, u32[]{:S(2)}) copy-start(s32[2,4]{1,0:T(2,128)} %param.20) | copy-start | bytes 100
  7.2 93.0 %copy-start.6 = (bf16[8,16,256]{2,1,0:T(8,128)(2,1)S(1)}, bf16[8,16,256]{2,1,0:T(8,128)(2,1)}, u32[]{:S(2)}) copy-start(bf16[8,16,256]{2,1,0:T(8,128)(2,1)} %param.18) | copy-start | bytes 196612
  7.2 149.2 %all-gather.5.cloned.1.call-start = ((), (), s32[]{:S(2)}) async-start(), calls=%async_computation.4 | async-start | bytes 1114112 | tf_op jit(solution)/shard_map/all_gather | solution.py:146
  8.8 92.0 %copy-start.7 = (bf16[8,16,256]{2,1,0:T(8,128)(2,1)S(1)}, bf16[8,16,256]{2,1,0:T(8,128)(2,1)}, u32[]{:S(2)}) copy-start(bf16[8,16,256]{2,1,0:T(8,128)(2,1)} %param.19) | copy-start | bytes 196612
  8.8 93.2 %copy-start.11 = (f32[2,3,256]{2,0,1:T(2,128)S(1)}, f32[2,3,256]{2,0,1:T(2,128)}, u32[]{:S(2)}) copy-start(f32[2,3,256]{2,0,1:T(2,128)} %param.23) | copy-start | bytes 18436
  8.9 93.2 %copy-start.12 = (f32[2,3,256]{2,0,1:T(2,128)S(1)}, f32[2,3,256]{2,0,1:T(2,128)}, u32[]{:S(2)}) copy-start(f32[2,3,256]{2,0,1:T(2,128)} %param.24) | copy-start | bytes 18436
  9.8 29.4 %all-to-all-start.2 = ((bf16[128,16,1,128]{3,0,2,1:T(8,128)(2,1)}), bf16[128,16,1,128]{3,0,2,1:T(8,128)(2,1)S(1)}, u32[]{:S(2)}, u32[]{:S(2)}) async-start(bf16[128,16,1,128]{3,0,2,1:T(8,128)(2,1)} %bitcast.16), calls=%async_computation.2 | async-start | bytes 1048576 | tf_op jit(solution)/shard_map/all_to_all | solution.py:114
  40.0 46.2 %all-to-all-start = ((bf16[128,16,1,128]{3,0,2,1:T(8,128)(2,1)}), bf16[128,16,1,128]{3,0,2,1:T(8,128)(2,1)S(1)}, u32[]{:S(2)}, u32[]{:S(2)}) async-start(bf16[128,16,1,128]{3,0,2,1:T(8,128)(2,1)} %bitcast.279), calls=%async_computation | async-start | bytes 1048576 | tf_op jit(solution)/shard_map/all_to_all | solution.py:113
  43.5 148.3 %all-gather.7.cloned.1.call-start = ((), (), s32[]{:S(2)}) async-start(), calls=%async_computation.5 | async-start | bytes 1114112 | tf_op jit(solution)/shard_map/all_gather | solution.py:147
  86.2 30.6 %all-to-all-start.1 = ((bf16[128,16,1,128]{0,3,2,1:T(8,128)(2,1)}), bf16[128,16,1,128]{0,3,2,1:T(8,128)(2,1)}, u32[]{:S(2)}, u32[]{:S(2)}) async-start(bf16[128,16,1,128]{0,3,2,1:T(8,128)(2,1)} %bitcast.278), calls=%async_computation.1 | async-start | bytes 1048576 | tf_op jit(solution)/shard_map/all_to_all | solution.py:112
  121.9 1.5 copy-start.2
  123.4 1.4 copy-start.1
  124.8 1.1 copy-start.3
  126.3 1.4 copy-start.5
  126.9 1.3 copy-start.4
  128.2 7.9 %copy-start.18 = (s32[64]{0:T(128)S(1)}, s32[64]{0:T(128)}, u32[]{:S(2)}) copy-start(s32[64]{0:T(128)} %add.158) | copy-start | bytes 772
  128.2 7.9 %copy-start.20 = (s32[2]{0:T(128)S(1)}, s32[2]{0:T(128)}, u32[]{:S(2)}) copy-start(s32[2]{0:T(128)} %param.21) | copy-start | bytes 28
  131.1 19.9 %all-to-all-start.3 = ((bf16[16,2,8192]{2,1,0:T(2,128)(2,1)}), bf16[16,2,8192]{2,1,0:T(2,128)(2,1)}, u32[]{:S(2)}, u32[]{:S(2)}) async-start(bf16[16,2,8192]{2,1,0:T(2,128)(2,1)} %reshape.478), calls=%async_computation.3 | async-start | bytes 1048576 | tf_op jit(solution)/shard_map/all_to_all | solution.py:119
  135.4 0.8 copy-start.15
  136.2 14.8 %copy-start.14 = (pred[2,64]{1,0:T(4,128)(4,1)}, pred[2,64]{1,0:T(4,128)(4,1)S(1)}, u32[]{:S(2)}) copy-start(pred[2,64]{1,0:T(4,128)(4,1)S(1)} %broadcast_compare_fusion) | copy-start | bytes 388
  153.2 4.6 %copy-start.10 = (pred[2048]{0:T(1024)(128)(4,1)S(1)}, pred[2048]{0:T(1024)(128)(4,1)}, u32[]{:S(2)}) copy-start(pred[2048]{0:T(1024)(128)(4,1)} %reshape.426) | copy-start | bytes 6148
  156.5 33.8 %copy-start.8 = (bf16[2,64,2,128]{3,2,1,0:T(2,128)(2,1)S(1)}, bf16[2,64,2,128]{3,2,1,0:T(2,128)(2,1)}, u32[]{:S(2)}) copy-start(bf16[2,64,2,128]{3,2,1,0:T(2,128)(2,1)} %reshape.428) | copy-start | bytes 196612
  191.8 23.6 %copy-start.13 = (f32[2,3,2,128]{3,2,0,1:T(2,128)S(1)}, f32[2,3,2,128]{3,2,0,1:T(2,128)}, u32[]{:S(2)}) copy-start(f32[2,3,2,128]{3,2,0,1:T(2,128)} %reshape.431) | copy-start | bytes 18436
  191.8 23.6 %copy-start.16 = (pred[3,3]{1,0:T(4,128)(4,1)S(1)}, pred[3,3]{1,0:T(4,128)(4,1)}, u32[]{:S(2)}) copy-start(pred[3,3]{1,0:T(4,128)(4,1)} %copy-done.15) | copy-start | bytes 31
Sparse Core Ops, SparseCore 0:
  10.1 79.2 all-gather.4
  91.5 82.2 all-gather.6
where the time goes:
time: 237 us; the launch traced here: 236 us
  blocking collectives  96.4 us (41%)
  waiting for transfers between devices  42.9 us (18%)
  starting transfers between devices  32.9 us (14%)
  local copies, waits for them, and re-layouts  28.1 us (12%)
  between operations  15.2 us (6%)
  matrix products  12.6 us (5%)
  other arithmetic  7.38 us (3%)
    all_gather x3, blocking collectives, merged(): everything = jax.tree.map(lambda part: lax.all_gather(part, axis), value)  47.9 us
    unnamed x1, blocking collectives  36.8 us
    all_to_all x1, waiting for transfers between devices, local(): lax.all_to_all(wide_v, 'seq', split_axis=1, concat_axis=0, tiled=True)  16.7 us
    all_to_all x1, waiting for transfers between devices, local(): lax.all_to_all(result, 'seq', split_axis=0, concat_axis=1, tiled=True)  14.3 us
    all_to_all x1, starting transfers between devices, local(): lax.all_to_all(wide_q, 'seq', split_axis=1, concat_axis=0, tiled=True)  13.2 us
    all_to_all x1, starting transfers between devices, local(): lax.all_to_all(wide_v, 'seq', split_axis=1, concat_axis=0, tiled=True)  11.8 us
    psum x1, blocking collectives, local(): lax.psum(projected, 'tp').reshape(requests, new_count, projected.shape[1])  11.7 us
    all_to_all x1, waiting for transfers between devices, local(): lax.all_to_all(wide_q, 'seq', split_axis=1, concat_axis=0, tiled=True)  10.6 us
  transfers between devices with their start and end apart: 6, of which 3 were waited for; matrix products, arithmetic and copies ran while one was open for 17% of the time, Pallas kernels for 0%

commit v1 on v0

v1 whole, which is shorter than its diff:
```python
import jax
import jax.numpy as jnp
from jax import lax
from jax.experimental import pallas as pl
from jax.experimental.pallas import tpu as pltpu
from jax.sharding import PartitionSpec as P

HD = 128
PAGE = 16
NEW = 3
SLOTS = 2
FLOOR = -1e30
SCALE = HD ** (-0.5)
LOG2E = 1.4426950408889634
ABSENT = 1024.0
KEY_BLOCK = 256

f32 = jnp.float32
bf16 = jnp.bfloat16
MIB = 1024 * 1024
VMEM = pl.BlockSpec(memory_space=pltpu.VMEM)
SMEM = pl.BlockSpec(memory_space=pltpu.SMEM)
NT = (((1,), (1,)), ((), ()))


def dot(a, b, dims=(((1,), (0,)), ((), ()))):
    return lax.dot_general(a, b, dims, preferred_element_type=f32)


def split(x, terms):
    out = []
    for _ in range(terms):
        part = x.astype(bf16)
        out.append(part)
        x = x - part.astype(f32)
    return out


def pack_kernel(owner_ref, k_ref, v_ref, send_ref):
    cols = k_ref.shape[1]
    pages = k_ref.shape[0] // PAGE
    send_ref[:, :, :cols] = jnp.full((send_ref.shape[0], SLOTS * PAGE, cols), ABSENT, bf16)
    send_ref[:, :, cols:] = jnp.zeros((send_ref.shape[0], SLOTS * PAGE, cols), bf16)
    owners = [owner_ref[j] for j in range(pages)]
    for j in range(pages):
        slot = jnp.int32(0)
        for i in range(j):
            slot = slot + (owners[i] == owners[j]).astype(jnp.int32)
        slot = jnp.minimum(slot, SLOTS - 1)
        rows = pl.ds(pl.multiple_of(slot * PAGE, PAGE), PAGE)
        send_ref[owners[j], rows, :cols] = k_ref[j * PAGE : (j + 1) * PAGE, :]
        send_ref[owners[j], rows, cols:] = v_ref[j * PAGE : (j + 1) * PAGE, :]


def decode_kernel(
    seq_ref, table_ref, length_ref, q_ref, recv_ref, ck_ref, cv_ref, dk_ref, dv_ref,
    out_ref, q_wide, pool_k, pool_v,
):
    seq = seq_ref[0]
    heads = q_ref.shape[1] // HD
    half = heads // 2
    cols = ck_ref.shape[2]
    requests, entries = table_ref.shape
    lanes = heads * 8
    q_wide[...] = jnp.zeros_like(q_wide)
    for h in range(heads):
        at = (h // half) * HD
        q_wide[h * 8 : (h + 1) * 8, at : at + HD] = q_ref[:, h * HD : (h + 1) * HD]
    for r in range(requests):
        for j in range(entries):
            rows = slice((r * entries + j) * PAGE, (r * entries + j + 1) * PAGE)
            page = table_ref[r, j]
            pool_k[rows, :] = ck_ref[page]
            pool_v[rows, :] = cv_ref[page]
    queries = split(q_wide[...], 3)

    def scores_of(keys):
        total = dot(keys, queries[0], NT)
        for part in queries[1:]:
            total = total + dot(keys, part, NT)
        return total * SCALE

    recv_rows = recv_ref.shape[0]
    recv_k = recv_ref[:, :cols]
    recv_scores = scores_of(recv_k)
    recv_valid = jnp.broadcast_to(recv_k[:, 0:1].astype(f32) < 0.5 * ABSENT, (recv_rows, lanes))
    pool_rows = requests * entries * PAGE
    key_at = lax.broadcasted_iota(jnp.int32, (pool_rows, lanes), 0)
    lane = lax.broadcasted_iota(jnp.int32, (pool_rows, lanes), 1)
    lane_request = (lane % 8 >= NEW).astype(jnp.int32)
    key_request = key_at // (entries * PAGE)
    local_at = key_at % (entries * PAGE)
    position = ((local_at // PAGE) * 16 + seq) * PAGE + local_at % PAGE
    length = jnp.where(key_request == 0, length_ref[0], length_ref[1])
    pool_valid = (position < length) & (lane_request == key_request)
    pool_scores = scores_of(pool_k[...])
    new_at = lax.broadcasted_iota(jnp.int32, (8, lanes), 0)
    new_lane = lax.broadcasted_iota(jnp.int32, (8, lanes), 1) % 8
    new_lane_request = (new_lane >= NEW).astype(jnp.int32)
    new_request = (new_at >= NEW).astype(jnp.int32)
    new_valid = (
        (new_at < requests * NEW)
        & (new_request == new_lane_request)
        & (new_at - new_request * NEW <= new_lane - new_lane_request * NEW)
        & (seq == 0)
    )
    new_scores = (
        lax.dot_general(
            dk_ref[...], q_wide[...], NT, precision=lax.Precision.HIGHEST,
            preferred_element_type=f32,
        )
        * SCALE
    )
    parts = [(recv_scores, recv_valid), (pool_scores, pool_valid), (new_scores, new_valid)]
    peak = jnp.full((1, lanes), FLOOR, f32)
    for scores, valid in parts:
        masked = jnp.where(valid, scores, FLOOR)
        peak = jnp.maximum(peak, jnp.max(masked, axis=0, keepdims=True))
    weights = [jnp.where(valid, jnp.exp(scores - peak), 0.0) for scores, valid in parts]
    total = jnp.zeros((1, lanes), f32)
    for w in weights:
        total = total + jnp.sum(w, axis=0, keepdims=True)
    mixed = jnp.zeros((lanes, cols), f32)
    for w, values in ((weights[0], recv_ref[:, cols:]), (weights[1], pool_v[...])):
        for part in split(w.T, 2):
            mixed = mixed + dot(part, values)
    new_w = jnp.concatenate([weights[2], jnp.zeros((lanes - 8, lanes), f32)], axis=0).T
    new_v = jnp.concatenate([dv_ref[...], jnp.zeros((lanes - 8, cols), f32)], axis=0)
    mixed = mixed + lax.dot_general(
        new_w, new_v, (((1,), (0,)), ((), ())), precision=lax.Precision.HIGHEST,
        preferred_element_type=f32,
    )
    out_ref[: half * 8, :] = mixed[: half * 8, :HD]
    out_ref[half * 8 :, :] = mixed[half * 8 :, HD:]
    out_ref[6:7, :] = peak
    out_ref[7:8, :] = total


def finish_kernel(all_ref, w_ref, out_ref, attention):
    count = all_ref.shape[0]
    lanes = all_ref.shape[1]
    heads = lanes // 8
    peaks = jnp.concatenate([all_ref[s, 6:7, :] for s in range(count)], axis=0)
    totals = jnp.concatenate([all_ref[s, 7:8, :] for s in range(count)], axis=0)
    factor = jnp.exp(peaks - jnp.max(peaks, axis=0, keepdims=True))
    share = factor / jnp.sum(factor * totals, axis=0, keepdims=True)
    share = jnp.concatenate([share, jnp.zeros((lanes - count, lanes), f32)], axis=0).T
    mixed = share[:, 0:1] * all_ref[0]
    for s in range(1, count):
        mixed = mixed + share[:, s : s + 1] * all_ref[s]
    row = lax.broadcasted_iota(jnp.int32, (8, HD), 0)
    for h in range(heads):
        attention[:, h * HD : (h + 1) * HD] = jnp.where(row < 6, mixed[h * 8 : (h + 1) * 8, :], 0.0)
    w = w_ref[...]
    result = jnp.zeros(out_ref.shape, f32)
    for part in split(attention[...], 3):
        result = result + dot(part, w)
    out_ref[...] = result


def prefill_kernel(seq_ref, q_ref, kv_ref, out_ref, q_rows, scores, peaks, sums, mixed):
    seq = seq_ref[0]
    tokens = q_ref.shape[0]
    heads = q_ref.shape[1] // HD
    group = heads // 2
    rows = group * tokens
    last = seq * tokens // KEY_BLOCK
    lanes_of = KEY_BLOCK // HD

    def fold(x, op):
        out = x[:, :HD]
        for i in range(1, lanes_of):
            out = op(out, x[:, i * HD : (i + 1) * HD])
        return out

    for k in range(2):
        for a in range(group):
            h = k * group + a
            q_rows[a * tokens : (a + 1) * tokens, :] = q_ref[:, h * HD : (h + 1) * HD]
        peaks[...] = jnp.full(peaks.shape, FLOOR, f32)

        def score_block(j, masked):
            at = pl.multiple_of(j * KEY_BLOCK, KEY_BLOCK)
            s = dot(q_rows[...], kv_ref[pl.ds(at, KEY_BLOCK), k * HD : (k + 1) * HD], NT)
            if masked:
                q_at = lax.broadcasted_iota(jnp.int32, s.shape, 0) % tokens + seq * tokens
                k_at = lax.broadcasted_iota(jnp.int32, s.shape, 1) + at
                s = jnp.where(k_at <= q_at, s, FLOOR)
            scores[j] = s
            peaks[...] = jnp.maximum(peaks[...], fold(s, jnp.maximum))

        def first(j, carry):
            score_block(j, False)
            return carry

        lax.fori_loop(0, last, first, 0)
        score_block(last, True)
        peak = jnp.max(peaks[...], axis=1, keepdims=True)
        peaks[...] = jnp.broadcast_to(peak, peaks.shape)
        sums[...] = jnp.zeros_like(sums)
        mixed[...] = jnp.zeros_like(mixed)

        def second(j, carry):
            at = pl.multiple_of(j * KEY_BLOCK, KEY_BLOCK)
            p = jnp.exp2((scores[j] - jnp.concatenate([peaks[...]] * lanes_of, axis=1)) * (SCALE * LOG2E))
            sums[...] += fold(p, jnp.add)
            mixed[...] += dot(
                p.astype(bf16), kv_ref[pl.ds(at, KEY_BLOCK), (2 + k) * HD : (3 + k) * HD]
            )
            return carry

        lax.fori_loop(0, last + 1, second, 0)
        result = (mixed[...] / jnp.sum(sums[...], axis=1, keepdims=True)).astype(bf16)
        for a in range(group):
            h = k * group + a
            out_ref[:, h * HD : (h + 1) * HD] = result[a * tokens : (a + 1) * tokens, :]


def local(
    pre_q, pre_k, pre_v, owner_map, cache_k, cache_v, tables, lengths, dec_q, dec_k, dec_v, w_out
):
    seq = lax.axis_index("seq").astype(jnp.int32).reshape(1)
    owners = lax.axis_size("batch")
    tokens, cols = pre_k.shape[1], pre_k.shape[2]
    requests, new, q_cols = dec_q.shape
    lanes = q_cols // HD * 8

    kv = jnp.concatenate([pre_k[0], pre_v[0]], axis=1)
    all_kv = lax.all_gather(kv, "seq", axis=0, tiled=True)

    send = pl.pallas_call(
        pack_kernel,
        out_shape=jax.ShapeDtypeStruct((owners, SLOTS * PAGE, 2 * cols), bf16),
        in_specs=[SMEM, VMEM, VMEM],
        out_specs=VMEM,
        name="pack_pages",
    )(owner_map.reshape(-1), pre_k[0], pre_v[0])
    received = lax.all_to_all(send, "batch", 0, 0, tiled=True)

    def rows8(x):
        x = x.reshape(requests * new, x.shape[-1])
        return jnp.pad(x, ((0, 8 - requests * new), (0, 0)))

    partial_state = pl.pallas_call(
        decode_kernel,
        out_shape=jax.ShapeDtypeStruct((lanes, HD), f32),
        in_specs=[SMEM, SMEM, SMEM] + [VMEM] * 6,
        out_specs=VMEM,
        scratch_shapes=[
            pltpu.VMEM((lanes, 2 * HD), f32),
            pltpu.VMEM((requests * tables.shape[1] * PAGE, cols), bf16),
            pltpu.VMEM((requests * tables.shape[1] * PAGE, cols), bf16),
        ],
        compiler_params=pltpu.CompilerParams(vmem_limit_bytes=16 * MIB),
        name="decode_partial",
    )(
        seq, tables, lengths, rows8(dec_q),
        received.reshape(owners * SLOTS * PAGE, 2 * cols),
        cache_k, cache_v, rows8(dec_k), rows8(dec_v),
    )
    gathered = lax.all_gather(partial_state, "seq")
    projected = pl.pallas_call(
        finish_kernel,
        out_shape=jax.ShapeDtypeStruct((8, w_out.shape[1]), f32),
        in_specs=[VMEM, VMEM],
        out_specs=VMEM,
        scratch_shapes=[pltpu.VMEM((8, q_cols), f32)],
        compiler_params=pltpu.CompilerParams(vmem_limit_bytes=16 * MIB),
        name="finish_decode",
    )(gathered, w_out)
    mine = projected[: requests * new]
    other = lax.ppermute(mine, "tp", [(0, 1), (1, 0)])

    span = all_kv.shape[0]
    group = q_cols // HD // 2
    flops = 4 * 2 * group * tokens * span * HD
    pre_q, all_kv, mine = lax.optimization_barrier((pre_q, all_kv, mine))
    pre_out = pl.pallas_call(
        prefill_kernel,
        out_shape=jax.ShapeDtypeStruct((tokens, q_cols), bf16),
        in_specs=[SMEM, VMEM, VMEM],
        out_specs=VMEM,
        scratch_shapes=[
            pltpu.VMEM((group * tokens, HD), bf16),
            pltpu.VMEM((span // KEY_BLOCK, group * tokens, KEY_BLOCK), f32),
            pltpu.VMEM((group * tokens, HD), f32),
            pltpu.VMEM((group * tokens, HD), f32),
            pltpu.VMEM((group * tokens, HD), f32),
        ],
        compiler_params=pltpu.CompilerParams(vmem_limit_bytes=32 * MIB),
        cost_estimate=pl.CostEstimate(
            flops=flops, bytes_accessed=4 * MIB, transcendentals=2 * group * tokens * span
        ),
        name="prefill_attention",
    )(seq, pre_q[0], all_kv)
    dec_out = (mine + other).reshape(requests, new, w_out.shape[1])
    return (pre_out[None], dec_out)


def solution(mesh):
    placed = (
        P("batch", "seq", "tp"),
        P("batch", "seq", "tp"),
        P("batch", "seq", "tp"),
        P("batch", "seq", None),
        P("batch", "seq", "tp"),
        P("batch", "seq", "tp"),
        P("batch", "seq"),
        P("batch"),
        P("batch", None, "tp"),
        P("batch", None, "tp"),
        P("batch", None, "tp"),
        P("tp", "seq"),
    )
    return jax.shard_map(
        local,
        mesh=mesh,
        in_specs=placed,
        out_specs=(P("batch", "seq", "tp"), P("batch", None, "seq")),
        check_vma=False,
    )
```

time: 237 us -> 135 us (0.57)
  blocking collectives: 96.4 us -> 0 us
  waiting for transfers between devices: 42.9 us -> 91 us
  local copies, waits for them, and re-layouts: 28.1 us -> 5.08 us
  starting transfers between devices: 32.9 us -> 15.2 us
  matrix products: 12.6 us -> 0 us
  Pallas kernels: 0 us -> 8.12 us
  other arithmetic: 7.38 us -> 0.67 us
    all_gather x2, waiting for transfers between devices: 0.01 us -> 80.2 us  [the longest x1 45.8 us: local(): gathered = lax.all_gather(partial_state, 'seq')]
    all_gather x3 -> x0, blocking collectives: 47.9 us -> none  [merged(): everything = jax.tree.map(lambda part: lax.all_gather(part, axis), value)]
    unnamed x1 -> x0, blocking collectives: 36.8 us -> none
    all_to_all x4 -> x1, waiting for transfers between devices: 41.5 us -> 10.7 us  [local(): received = lax.all_to_all(send, 'batch', 0, 0, tiled=True)]
    all_to_all x4 -> x1, starting transfers between devices: 32.8 us -> 7.99 us  [local(): received = lax.all_to_all(send, 'batch', 0, 0, tiled=True)]
    dot_general x15 -> x0, matrix products: 12.6 us -> none  [the longest x3 3.68 us: partial_state(): jnp.einsum(pattern, weights, value_rows, precision=highest)]
    psum x1 -> x0, blocking collectives: 11.7 us -> none  [local(): lax.psum(projected, 'tp').reshape(requests, new_count, projected.shape[1])]
    pallas_call x0 -> x4, Pallas kernels: none -> 8.12 us  [the longest x1 2.77 us: local(): pl.pallas_call(prefill_kernel, out_shape=jax.ShapeDtypeStruct((tokens, q_...]
  transfers between devices with their start and end apart: 6 -> 4, of which waited for: 3 -> 3; matrix products, arithmetic and copies ran while one was open for 17% -> 2% of each run, Pallas kernels for 0% -> 1%
where the time goes in v1:
time: 135 us; the launch traced here: 134 us
  waiting for transfers between devices  91 us (67%)
  starting transfers between devices  15.2 us (11%)
  between operations  14.2 us (11%)
  Pallas kernels  8.12 us (6%)
  local copies, waits for them, and re-layouts  5.08 us (4%)
    all_gather x1, waiting for transfers between devices, local(): gathered = lax.all_gather(partial_state, 'seq')  45.8 us
    all_gather x1, waiting for transfers between devices, local(): all_kv = lax.all_gather(kv, 'seq', axis=0, tiled=True)  34.4 us
    all_to_all x1, waiting for transfers between devices, local(): received = lax.all_to_all(send, 'batch', 0, 0, tiled=True)  10.7 us
    all_to_all x1, starting transfers between devices, local(): received = lax.all_to_all(send, 'batch', 0, 0, tiled=True)  7.99 us
    ppermute x1, starting transfers between devices, local(): other = lax.ppermute(mine, 'tp', [(0, 1), (1, 0)])  7.08 us
    unnamed x26, local copies, waits for them, and re-layouts  5 us
    pallas_call x1, Pallas kernels, local(): pl.pallas_call(prefill_kernel, out_shape=jax.ShapeDtypeStruct((tokens, q_...  2.77 us
  transfers between devices with their start and end apart: 4, of which 3 were waited for; matrix products, arithmetic and copies ran while one was open for 2% of the time, Pallas kernels for 1%

profile of v1, /device:TPU:1, one launch (start us, length us, event | category | flops | bytes accessed | tf_op | source)
XLA Modules:
  0.0 134.2 jit_solution(16368282295212323590)
XLA Ops:
  7.2 0.0 copy-start.8
  7.2 0.0 copy-start.9
  7.2 0.0 copy-start.10
  7.2 0.0 copy-start.2
  7.2 0.0 copy-start.3
  7.2 0.0 copy-start.4
  7.2 0.0 copy-start.5
  7.2 0.0 copy-start
  7.2 1.9 %pack_pages.1 = bf16[16,32,512]{2,1,0:T(8,128)(2,1)} custom-call(s32[8]{0:T(128)} %bitcast.18, bf16[128,256]{1,0:T(8,128)(2,1)} %bitcast.14, bf16[128,256]{1,0:T(8,128)(2,1)} %bitcast.16), custom_call_target="tpu_custom_call" | custom-call | tf_op jit(solution)/shard_map/pack_pages/pallas_call | solution.py:231
  9.1 8.0 %all-to-all-start = ((bf16[16,32,512]{2,1,0:T(8,128)(2,1)}), bf16[16,32,512]{2,1,0:T(8,128)(2,1)S(1)}, u32[]{:S(2)}, u32[]{:S(2)}) async-start(bf16[16,32,512]{2,1,0:T(8,128)(2,1)} %pack_pages.1), calls=%async_computation | async-start | bytes 1048576 | tf_op jit(solution)/shard_map/all_to_all | solution.py:238
  17.1 0.0 all-gather.6.cloned.1.call-start
  17.2 0.8 copy.18
  18.1 0.7 copy.19
  18.8 0.0 copy-done.10
  18.8 10.7 %all-to-all-done = bf16[16,32,512]{2,1,0:T(8,128)(2,1)S(1)} async-done(((bf16[16,32,512]{2,1,0:T(8,128)(2,1)}), bf16[16,32,512]{2,1,0:T(8,128)(2,1)S(1)}, u32[]{:S(2)}, u32[]{:S(2)}) %all-to-all-start) | async-done | bytes 524320 | tf_op jit(solution)/shard_map/all_to_all | solution.py:238
  29.6 0.0 copy-done.2
  29.6 0.0 copy-done.3
  29.6 0.0 copy-done.4
  29.6 0.0 copy-done.5
  29.6 0.0 copy-start.7
  29.6 2.2 %decode_partial.1 = f32[128,128]{1,0:T(8,128)} custom-call(s32[1]{0:T(128)} %bitcast.seq_ref, s32[2,4]{1,0:T(2,128)S(1)} %copy-done.4, s32[2]{0:T(128)S(1)} %copy-done.5, f32[8,2048]{1,0:T(8,128)S(1)} %pad.11.q_ref, bf16[512,512]{1,0:T(8,128)(2,1)S(1)} %bitcast.9, bf16[8,16,256]{2,1,0:T(8,128)(2,1)S(1)} %copy-done.2, bf16[8,16,256]{2,1,0:T(8,128)(2,1)S(1)} %copy-done.3, ...), custom_call_target="tpu_custom_call" | custom-call | tf_op jit(solution)/shard_map/decode_partial/pallas_call | solution.py:244
  31.8 0.0 all-gather.6.cloned.1.call-update
  31.8 0.0 all-gather.4.cloned.1.call-start
  31.9 0.0 copy-done.8
  31.9 0.0 copy-done.9
  31.9 0.7 pad_maximum_fusion
  32.5 0.0 all-gather.4.cloned.1.call-update
  32.6 45.8 %all-gather.6.cloned.1.call-done = f32[2048,128]{1,0:T(8,128)} async-done(((f32[128,128]{1,0:T(8,128)}), f32[2048,128]{1,0:T(8,128)}) %all-gather.6.cloned.1.call-update) | async-done | bytes 1048592 | tf_op jit(solution)/shard_map/all_gather | solution.py:261
  78.4 0.0 copy-done
  78.4 0.0 copy-start.1
  78.4 1.2 copy-done.1
  79.6 1.3 finish_decode.1
  80.9 7.1 %collective-permute-start = (f32[6,512]{1,0:T(8,128)S(1)}, f32[6,512]{1,0:T(8,128)S(1)}, u32[]{:S(2)}, u32[]{:S(2)}) collective-permute-start(f32[6,512]{1,0:T(8,128)S(1)} %bitcast.11), channel_id=1, source_target_pairs={{0,1},{1,0},{2,3},{3,2},{4,5},{5,4},{6,7},{7,6},{8,9},{9,8},{10,11... | collective-permute-start | bytes 36872 | tf_op jit(solution)/shard_map/ppermute | solution.py:272
  88.0 34.4 %all-gather.4.cloned.1.call-done.kv_ref = bf16[2048,512]{1,0:T(8,128)(2,1)} async-done(((bf16[128,512]{1,0:T(8,128)(2,1)}), bf16[2048,512]{1,0:T(8,128)(2,1)}) %all-gather.4.cloned.1.call-update) | async-done | bytes 2097168 | tf_op jit(solution)/shard_map/all_gather | solution.py:229
  122.4 0.0 collective-permute-done
  122.4 0.6 copy.21
  123.0 0.0 copy-done.7
  123.0 0.0 copy-start.6
  123.0 1.6 %copy-done.6 = bf16[2048,512]{1,0:T(8,128)(2,1)S(1)} copy-done((bf16[2048,512]{1,0:T(8,128)(2,1)S(1)}, bf16[2048,512]{1,0:T(8,128)(2,1)}, u32[]{:S(2)}) %copy-start.6) | copy-done | bytes 2097176
  124.6 2.8 %prefill_attention.1 = bf16[128,2048]{1,0:T(8,128)(2,1)} custom-call(s32[1]{0:T(128)} %bitcast.seq_ref, bf16[128,2048]{1,0:T(8,128)(2,1)S(1)} %bitcast.13, bf16[2048,512]{1,0:T(8,128)(2,1)S(1)} %copy-done.6), custom_call_target="tpu_custom_call" | custom-call | flops 2147483648 | bytes 4194304 | tf_op jit(solution)/shard_map/prefill_attention/pallas_call | solution.py:278
  (9 shorter events, 0.1 us)
Async XLA Ops:
  7.2 24.7 %copy-start.8 = (bf16[1,128,256]{2,1,0:T(8,128)(2,1)S(1)}, bf16[1,128,256]{2,1,0:T(8,128)(2,1)}, u32[]{:S(2)}) copy-start(bf16[1,128,256]{2,1,0:T(8,128)(2,1)} %param.13) | copy-start | bytes 196612
  7.2 24.7 %copy-start.9 = (bf16[1,128,256]{2,1,0:T(8,128)(2,1)S(1)}, bf16[1,128,256]{2,1,0:T(8,128)(2,1)}, u32[]{:S(2)}) copy-start(bf16[1,128,256]{2,1,0:T(8,128)(2,1)} %param.14) | copy-start | bytes 196612
  7.2 11.6 %copy-start.10 = (f32[2,3,256]{2,0,1:T(2,128)S(1)}, f32[2,3,256]{2,0,1:T(2,128)}, u32[]{:S(2)}) copy-start(f32[2,3,256]{2,0,1:T(2,128)} %param.22) | copy-start | bytes 18436
  7.2 22.4 %copy-start.2 = (bf16[8,16,256]{2,1,0:T(8,128)(2,1)S(1)}, bf16[8,16,256]{2,1,0:T(8,128)(2,1)}, u32[]{:S(2)}) copy-start(bf16[8,16,256]{2,1,0:T(8,128)(2,1)} %ck_ref.1) | copy-start | bytes 196612
  7.2 22.4 %copy-start.3 = (bf16[8,16,256]{2,1,0:T(8,128)(2,1)S(1)}, bf16[8,16,256]{2,1,0:T(8,128)(2,1)}, u32[]{:S(2)}) copy-start(bf16[8,16,256]{2,1,0:T(8,128)(2,1)} %cv_ref.1) | copy-start | bytes 196612
  7.2 22.4 %copy-start.4 = (s32[2,4]{1,0:T(2,128)S(1)}, s32[2,4]{1,0:T(2,128)}, u32[]{:S(2)}) copy-start(s32[2,4]{1,0:T(2,128)} %table_ref.1) | copy-start | bytes 100
  7.2 22.4 %copy-start.5 = (s32[2]{0:T(128)S(1)}, s32[2]{0:T(128)}, u32[]{:S(2)}) copy-start(s32[2]{0:T(128)} %length_ref.1) | copy-start | bytes 28
  7.2 71.1 %copy-start = (bf16[2048,512]{1,0:T(8,128)(2,1)S(1)}, bf16[2048,512]{1,0:T(8,128)(2,1)}, u32[]{:S(2)}) copy-start(bf16[2048,512]{1,0:T(8,128)(2,1)} %w_ref.1) | copy-start | bytes 6291460
  9.1 20.4 %all-to-all-start = ((bf16[16,32,512]{2,1,0:T(8,128)(2,1)}), bf16[16,32,512]{2,1,0:T(8,128)(2,1)S(1)}, u32[]{:S(2)}, u32[]{:S(2)}) async-start(bf16[16,32,512]{2,1,0:T(8,128)(2,1)} %pack_pages.1), calls=%async_computation | async-start | bytes 1048576 | tf_op jit(solution)/shard_map/all_to_all | solution.py:238
  17.1 61.2 %all-gather.6.cloned.1.call-start = ((), (), s32[]{:S(2)}) async-start(), calls=%async_computation.2 | async-start | bytes 1114112 | tf_op jit(solution)/shard_map/all_gather | solution.py:261
  29.6 93.5 %copy-start.7 = (bf16[1,128,2048]{2,1,0:T(8,128)(2,1)S(1)}, bf16[1,128,2048]{2,1,0:T(8,128)(2,1)}, u32[]{:S(2)}) copy-start(bf16[1,128,2048]{2,1,0:T(8,128)(2,1)} %param.12) | copy-start | bytes 1572868
  31.8 90.6 %all-gather.4.cloned.1.call-start = ((), (), s32[]{:S(2)}) async-start(), calls=%async_computation.1 | async-start | bytes 2228224 | tf_op jit(solution)/shard_map/all_gather | solution.py:229
  78.4 1.2 copy-start.1
  80.9 41.5 %collective-permute-start = (f32[6,512]{1,0:T(8,128)S(1)}, f32[6,512]{1,0:T(8,128)S(1)}, u32[]{:S(2)}, u32[]{:S(2)}) collective-permute-start(f32[6,512]{1,0:T(8,128)S(1)} %bitcast.11), channel_id=1, source_target_pairs={{0,1},{1,0},{2,3},{3,2},{4,5},{5,4},{6,7},{7,6},{8,9},{9,8},{10,11... | collective-permute-start | bytes 36872 | tf_op jit(solution)/shard_map/ppermute | solution.py:272
  123.0 1.6 %copy-start.6 = (bf16[2048,512]{1,0:T(8,128)(2,1)S(1)}, bf16[2048,512]{1,0:T(8,128)(2,1)}, u32[]{:S(2)}) copy-start(bf16[2048,512]{1,0:T(8,128)(2,1)} %all-gather.4.cloned.1.call-done.kv_ref) | copy-start | bytes 6291460
Sparse Core Ops, SparseCore 0:
  31.9 46.4 all-gather.5
  81.1 41.2 all-gather.3

commit v2 on v1

--- a/solution.py
+++ b/solution.py
@@ -36,11 +36,13 @@
     return out
 
 
-def pack_kernel(owner_ref, k_ref, v_ref, send_ref):
+def pack_kernel(owner_ref, k_ref, v_ref, send_ref, kv_ref):
     cols = k_ref.shape[1]
     pages = k_ref.shape[0] // PAGE
     send_ref[:, :, :cols] = jnp.full((send_ref.shape[0], SLOTS * PAGE, cols), ABSENT, bf16)
     send_ref[:, :, cols:] = jnp.zeros((send_ref.shape[0], SLOTS * PAGE, cols), bf16)
+    kv_ref[:, :cols] = k_ref[...]
+    kv_ref[:, cols:] = v_ref[...]
     owners = [owner_ref[j] for j in range(pages)]
     for j in range(pages):
         slot = jnp.int32(0)
@@ -61,11 +63,13 @@
     half = heads // 2
     cols = ck_ref.shape[2]
     requests, entries = table_ref.shape
-    lanes = heads * 8
+    each = requests * NEW
+    rows_used = heads * each
+    lanes = q_wide.shape[0]
     q_wide[...] = jnp.zeros_like(q_wide)
     for h in range(heads):
         at = (h // half) * HD
-        q_wide[h * 8 : (h + 1) * 8, at : at + HD] = q_ref[:, h * HD : (h + 1) * HD]
+        q_wide[h * each : (h + 1) * each, at : at + HD] = q_ref[:each, h * HD : (h + 1) * HD]
     for r in range(requests):
         for j in range(entries):
             rows = slice((r * entries + j) * PAGE, (r * entries + j + 1) * PAGE)
@@ -87,7 +91,7 @@
     pool_rows = requests * entries * PAGE
     key_at = lax.broadcasted_iota(jnp.int32, (pool_rows, lanes), 0)
     lane = lax.broadcasted_iota(jnp.int32, (pool_rows, lanes), 1)
-    lane_request = (lane % 8 >= NEW).astype(jnp.int32)
+    lane_request = (lane % each >= NEW).astype(jnp.int32)
     key_request = key_at // (entries * PAGE)
     local_at = key_at % (entries * PAGE)
     position = ((local_at // PAGE) * 16 + seq) * PAGE + local_at % PAGE
@@ -95,11 +99,11 @@
     pool_valid = (position < length) & (lane_request == key_request)
     pool_scores = scores_of(pool_k[...])
     new_at = lax.broadcasted_iota(jnp.int32, (8, lanes), 0)
-    new_lane = lax.broadcasted_iota(jnp.int32, (8, lanes), 1) % 8
+    new_lane = lax.broadcasted_iota(jnp.int32, (8, lanes), 1) % each
     new_lane_request = (new_lane >= NEW).astype(jnp.int32)
     new_request = (new_at >= NEW).astype(jnp.int32)
     new_valid = (
-        (new_at < requests * NEW)
+        (new_at < each)
         & (new_request == new_lane_request)
         & (new_at - new_request * NEW <= new_lane - new_lane_request * NEW)
         & (seq == 0)
@@ -130,27 +134,31 @@
         new_w, new_v, (((1,), (0,)), ((), ())), precision=lax.Precision.HIGHEST,
         preferred_element_type=f32,
     )
-    out_ref[: half * 8, :] = mixed[: half * 8, :HD]
-    out_ref[half * 8 :, :] = mixed[half * 8 :, HD:]
-    out_ref[6:7, :] = peak
-    out_ref[7:8, :] = total
+    out_ref[: half * each, :] = mixed[: half * each, :HD]
+    out_ref[half * each : rows_used, :] = mixed[half * each : rows_used, HD:]
+    out_ref[rows_used : rows_used + 1, :] = peak
+    out_ref[rows_used + 1 : rows_used + 2, :] = total
+    out_ref[rows_used + 2 :, :] = jnp.zeros((out_ref.shape[0] - rows_used - 2, HD), f32)
 
 
 def finish_kernel(all_ref, w_ref, out_ref, attention):
     count = all_ref.shape[0]
-    lanes = all_ref.shape[1]
-    heads = lanes // 8
-    peaks = jnp.concatenate([all_ref[s, 6:7, :] for s in range(count)], axis=0)
-    totals = jnp.concatenate([all_ref[s, 7:8, :] for s in range(count)], axis=0)
+    heads = attention.shape[1] // HD
+    rows_used = all_ref.shape[1] - 8
+    each = rows_used // heads
+    peaks = jnp.concatenate([all_ref[s, rows_used : rows_used + 1, :] for s in range(count)], axis=0)
+    totals = jnp.concatenate(
+        [all_ref[s, rows_used + 1 : rows_used + 2, :] for s in range(count)], axis=0
+    )
     factor = jnp.exp(peaks - jnp.max(peaks, axis=0, keepdims=True))
     share = factor / jnp.sum(factor * totals, axis=0, keepdims=True)
-    share = jnp.concatenate([share, jnp.zeros((lanes - count, lanes), f32)], axis=0).T
-    mixed = share[:, 0:1] * all_ref[0]
+    share = jnp.concatenate([share, jnp.zeros((HD - count, HD), f32)], axis=0).T[:rows_used]
+    mixed = share[:, 0:1] * all_ref[0, :rows_used, :]
     for s in range(1, count):
-        mixed = mixed + share[:, s : s + 1] * all_ref[s]
-    row = lax.broadcasted_iota(jnp.int32, (8, HD), 0)
+        mixed = mixed + share[:, s : s + 1] * all_ref[s, :rows_used, :]
+    attention[...] = jnp.zeros_like(attention)
     for h in range(heads):
-        attention[:, h * HD : (h + 1) * HD] = jnp.where(row < 6, mixed[h * 8 : (h + 1) * 8, :], 0.0)
+        attention[:each, h * HD : (h + 1) * HD] = mixed[h * each : (h + 1) * each, :]
     w = w_ref[...]
     result = jnp.zeros(out_ref.shape, f32)
     for part in split(attention[...], 3):
@@ -223,18 +231,19 @@
     owners = lax.axis_size("batch")
     tokens, cols = pre_k.shape[1], pre_k.shape[2]
     requests, new, q_cols = dec_q.shape
-    lanes = q_cols // HD * 8
-
-    kv = jnp.concatenate([pre_k[0], pre_v[0]], axis=1)
-    all_kv = lax.all_gather(kv, "seq", axis=0, tiled=True)
-
-    send = pl.pallas_call(
+    rows_used = q_cols // HD * requests * new
+
+    send, kv = pl.pallas_call(
         pack_kernel,
-        out_shape=jax.ShapeDtypeStruct((owners, SLOTS * PAGE, 2 * cols), bf16),
+        out_shape=(
+            jax.ShapeDtypeStruct((owners, SLOTS * PAGE, 2 * cols), bf16),
+            jax.ShapeDtypeStruct((tokens, 2 * cols), bf16),
+        ),
         in_specs=[SMEM, VMEM, VMEM],
-        out_specs=VMEM,
+        out_specs=(VMEM, VMEM),
         name="pack_pages",
     )(owner_map.reshape(-1), pre_k[0], pre_v[0])
+    all_kv = lax.all_gather(kv, "seq", axis=0, tiled=True)
     received = lax.all_to_all(send, "batch", 0, 0, tiled=True)
 
     def rows8(x):
@@ -243,11 +252,11 @@
 
     partial_state = pl.pallas_call(
         decode_kernel,
-        out_shape=jax.ShapeDtypeStruct((lanes, HD), f32),
+        out_shape=jax.ShapeDtypeStruct((rows_used + 8, HD), f32),
         in_specs=[SMEM, SMEM, SMEM] + [VMEM] * 6,
         out_specs=VMEM,
         scratch_shapes=[
-            pltpu.VMEM((lanes, 2 * HD), f32),
+            pltpu.VMEM((HD, 2 * HD), f32),
             pltpu.VMEM((requests * tables.shape[1] * PAGE, cols), bf16),
             pltpu.VMEM((requests * tables.shape[1] * PAGE, cols), bf16),
         ],
@@ -259,6 +268,7 @@
         cache_k, cache_v, rows8(dec_k), rows8(dec_v),
     )
     gathered = lax.all_gather(partial_state, "seq")
+    gathered, all_kv = lax.optimization_barrier((gathered, all_kv))
     projected = pl.pallas_call(
         finish_kernel,
         out_shape=jax.ShapeDtypeStruct((8, w_out.shape[1]), f32),

time: 135 us -> 82 us (0.61)
  waiting for transfers between devices: 91 us -> 10.1 us
  blocking collectives: 0 us -> 30.1 us
  starting transfers between devices: 15.2 us -> 13.8 us
    all_gather x1 -> x0, waiting for transfers between devices: 45.8 us -> none  [local(): gathered = lax.all_gather(partial_state, 'seq')]
    all_gather x1, waiting for transfers between devices: 34.4 us -> 0.01 us  [local(): all_kv = lax.all_gather(kv, 'seq', axis=0, tiled=True)]
    all_gather x0 -> x1, blocking collectives: none -> 30.1 us  [local(): gathered = lax.all_gather(partial_state, 'seq')]
    ppermute x1, starting transfers between devices: 7.08 us -> 5.72 us  [local(): other = lax.ppermute(mine, 'tp', [(0, 1), (1, 0)])]
    unnamed x26 -> x18, local copies, waits for them, and re-layouts: 5 us -> 5.86 us
  transfers between devices with their start and end apart: 4 -> 3, of which waited for: 3 -> 1; matrix products, arithmetic and copies ran while one was open for 2% -> 3% of each run, Pallas kernels for 1% -> 5%
where the time goes in v2:
time: 82 us; the launch traced here: 81.5 us
  blocking collectives  30.1 us (37%)
  between operations  14.1 us (17%)
  starting transfers between devices  13.8 us (17%)
  waiting for transfers between devices  10.1 us (12%)
  Pallas kernels  7.48 us (9%)
  local copies, waits for them, and re-layouts  5.95 us (7%)
    all_gather x1, blocking collectives, local(): gathered = lax.all_gather(partial_state, 'seq')  30.1 us
    all_to_all x1, waiting for transfers between devices, local(): received = lax.all_to_all(send, 'batch', 0, 0, tiled=True)  10.1 us
    all_to_all x1, starting transfers between devices, local(): received = lax.all_to_all(send, 'batch', 0, 0, tiled=True)  8 us
    unnamed x18, local copies, waits for them, and re-layouts  5.86 us
    ppermute x1, starting transfers between devices, local(): other = lax.ppermute(mine, 'tp', [(0, 1), (1, 0)])  5.72 us
    pallas_call x1, Pallas kernels, local(): pl.pallas_call(prefill_kernel, out_shape=jax.ShapeDtypeStruct((tokens, q_...  2.78 us
    pallas_call x1, Pallas kernels, local(): pl.pallas_call(pack_kernel, out_shape=(jax.ShapeDtypeStruct((owners, SLOT...  1.93 us
  transfers between devices with their start and end apart: 3, of which 1 were waited for; matrix products, arithmetic and copies ran while one was open for 3% of the time, Pallas kernels for 5%

profile of v2, /device:TPU:1, one launch (start us, length us, event | category | flops | bytes accessed | tf_op | source)
XLA Modules:
  0.0 81.5 jit_solution(1819891200348304036)
XLA Ops:
  7.2 0.0 copy-start
  7.2 0.0 all-gather.3.cloned.1.call-start
  7.2 1.9 %pack_pages.1 = (bf16[16,32,512]{2,1,0:T(8,128)(2,1)}, bf16[128,512]{1,0:T(8,128)(2,1)}) custom-call(s32[8]{0:T(128)} %bitcast.16, bf16[128,256]{1,0:T(8,128)(2,1)} %bitcast.14, bf16[128,256]{1,0:T(8,128)(2,1)} %bitcast.15), custom_call_target="tpu_custom_call" | custom-call | tf_op jit(solution)/shard_map/pack_pages/pallas_call | solution.py:236
  9.1 0.0 all-gather.3.cloned.1.call-update
  9.2 8.0 %all-to-all-start = ((bf16[16,32,512]{2,1,0:T(8,128)(2,1)}), bf16[16,32,512]{2,1,0:T(8,128)(2,1)S(1)}, u32[]{:S(2)}, u32[]{:S(2)}) async-start(bf16[16,32,512]{2,1,0:T(8,128)(2,1)} %get-tuple-element.9), calls=%async_computation | async-start | bytes 1048576 | tf_op jit(solution)/shard_map/all_to_all | solution.py:247
  17.2 0.8 %copy.18 = f32[2,3,2048]{2,1,0:T(4,128)S(1)} copy(f32[2,3,2048]{2,0,1:T(2,128)} %param.20) | data formatting | bytes 98304 | tf_op args[8]
  18.1 0.7 copy.19
  18.8 0.7 copy.20
  19.5 10.1 %all-to-all-done = bf16[16,32,512]{2,1,0:T(8,128)(2,1)S(1)} async-done(((bf16[16,32,512]{2,1,0:T(8,128)(2,1)}), bf16[16,32,512]{2,1,0:T(8,128)(2,1)S(1)}, u32[]{:S(2)}, u32[]{:S(2)}) %all-to-all-start) | async-done | bytes 524320 | tf_op jit(solution)/shard_map/all_to_all | solution.py:247
  29.6 0.0 copy-start.1
  29.6 0.8 %copy-done.1 = bf16[8,16,256]{2,1,0:T(8,128)(2,1)S(1)} copy-done((bf16[8,16,256]{2,1,0:T(8,128)(2,1)S(1)}, bf16[8,16,256]{2,1,0:T(8,128)(2,1)}, u32[]{:S(2)}) %copy-start.1) | copy-done | bytes 65560
  30.5 0.0 copy-start.2
  30.5 0.8 %copy-done.2 = bf16[8,16,256]{2,1,0:T(8,128)(2,1)S(1)} copy-done((bf16[8,16,256]{2,1,0:T(8,128)(2,1)S(1)}, bf16[8,16,256]{2,1,0:T(8,128)(2,1)}, u32[]{:S(2)}) %copy-start.2) | copy-done | bytes 65560
  31.3 0.0 copy-start.3
  31.3 0.7 copy-done.3
  32.0 0.0 copy-start.4
  32.0 0.7 copy-done.4
  32.6 1.6 %decode_partial.1 = f32[104,128]{1,0:T(8,128)S(1)} custom-call(s32[1]{0:T(128)} %bitcast.seq_ref, s32[2,4]{1,0:T(2,128)S(1)} %copy-done.3, s32[2]{0:T(128)S(1)} %copy-done.4, f32[8,2048]{1,0:T(8,128)S(1)} %pad.11.q_ref, bf16[512,512]{1,0:T(8,128)(2,1)S(1)} %bitcast.10, bf16[8,16,256]{2,1,0:T(8,128)(2,1)S(1)} %copy-done.1, bf16[8,16,256]{2,1,0:T(8,128)(2,1)S(1)} %copy-done.2, ...), custom_call_target="tpu_custom_call" | custom-call | tf_op jit(solution)/shard_map/decode_partial/pallas_call | solution.py:253
  34.2 0.0 copy-start.6
  34.2 30.1 %all-gather = f32[1664,128]{1,0:T(8,128)S(1)} all-gather(f32[104,128]{1,0:T(8,128)S(1)} %decode_partial.1), channel_id=2, replica_groups=mesh['seq'=16,'batch'=16,'tp'=2] {'seq'}, dimensions={0}, use_global_device_ids=true | all-gather | bytes 905216 | tf_op jit(solution)/shard_map/all_gather | solution.py:270
  64.3 0.0 all-gather.3.cloned.1.call-done.kv_ref
  64.3 0.0 copy-start.5
  64.3 0.0 copy-done
  64.3 1.2 %finish_decode.1 = f32[8,512]{1,0:T(8,128)S(1)} custom-call(f32[16,104,128]{2,1,0:T(8,128)S(1)} %bitcast.9, bf16[2048,512]{1,0:T(8,128)(2,1)S(1)} %copy-done), custom_call_target="tpu_custom_call" | custom-call | tf_op jit(solution)/shard_map/finish_decode/pallas_call | solution.py:272
  65.5 5.7 %collective-permute-start = (f32[6,512]{1,0:T(8,128)S(1)}, f32[6,512]{1,0:T(8,128)S(1)}, u32[]{:S(2)}, u32[]{:S(2)}) collective-permute-start(f32[6,512]{1,0:T(8,128)S(1)} %bitcast.11), channel_id=1, source_target_pairs={{0,1},{1,0},{2,3},{3,2},{4,5},{5,4},{6,7},{7,6},{8,9},{9,8},{10,11... | collective-permute-start | bytes 36872 | tf_op jit(solution)/shard_map/ppermute | solution.py:282
  71.2 0.0 copy-done.6
  71.3 0.0 copy-done.5
  71.3 2.8 %prefill_attention.1 = bf16[128,2048]{1,0:T(8,128)(2,1)} custom-call(s32[1]{0:T(128)} %bitcast.seq_ref, bf16[128,2048]{1,0:T(8,128)(2,1)S(1)} %bitcast.13, bf16[2048,512]{1,0:T(8,128)(2,1)S(1)} %copy-done.5), custom_call_target="tpu_custom_call" | custom-call | flops 2147483648 | bytes 4194304 | tf_op jit(solution)/shard_map/prefill_attention/pallas_call | solution.py:288
  74.0 0.0 collective-permute-done
  74.1 0.6 copy.21
  (8 shorter events, 0.1 us)
Async XLA Ops:
  7.2 57.2 %copy-start = (bf16[2048,512]{1,0:T(8,128)(2,1)S(1)}, bf16[2048,512]{1,0:T(8,128)(2,1)}, u32[]{:S(2)}) copy-start(bf16[2048,512]{1,0:T(8,128)(2,1)} %w_ref.1) | copy-start | bytes 6291460
  7.2 57.1 %all-gather.3.cloned.1.call-start = ((), (), s32[]{:S(2)}) async-start(), calls=%async_computation.1 | async-start | bytes 2228224 | tf_op jit(solution)/shard_map/all_gather | solution.py:246
  9.2 20.4 %all-to-all-start = ((bf16[16,32,512]{2,1,0:T(8,128)(2,1)}), bf16[16,32,512]{2,1,0:T(8,128)(2,1)S(1)}, u32[]{:S(2)}, u32[]{:S(2)}) async-start(bf16[16,32,512]{2,1,0:T(8,128)(2,1)} %get-tuple-element.9), calls=%async_computation | async-start | bytes 1048576 | tf_op jit(solution)/shard_map/all_to_all | solution.py:247
  29.6 0.8 %copy-start.1 = (bf16[8,16,256]{2,1,0:T(8,128)(2,1)S(1)}, bf16[8,16,256]{2,1,0:T(8,128)(2,1)}, u32[]{:S(2)}) copy-start(bf16[8,16,256]{2,1,0:T(8,128)(2,1)} %ck_ref.1) | copy-start | bytes 196612
  30.5 0.8 %copy-start.2 = (bf16[8,16,256]{2,1,0:T(8,128)(2,1)S(1)}, bf16[8,16,256]{2,1,0:T(8,128)(2,1)}, u32[]{:S(2)}) copy-start(bf16[8,16,256]{2,1,0:T(8,128)(2,1)} %cv_ref.1) | copy-start | bytes 196612
  31.3 0.7 copy-start.3
  32.0 0.7 copy-start.4
  34.2 37.0 %copy-start.6 = (bf16[1,128,2048]{2,1,0:T(8,128)(2,1)S(1)}, bf16[1,128,2048]{2,1,0:T(8,128)(2,1)}, u32[]{:S(2)}) copy-start(bf16[1,128,2048]{2,1,0:T(8,128)(2,1)} %param.12) | copy-start | bytes 1572868
  64.3 6.9 %copy-start.5 = (bf16[2048,512]{1,0:T(8,128)(2,1)S(1)}, bf16[2048,512]{1,0:T(8,128)(2,1)}, u32[]{:S(2)}) copy-start(bf16[2048,512]{1,0:T(8,128)(2,1)} %all-gather.3.cloned.1.call-done.kv_ref) | copy-start | bytes 6291460
  65.5 8.5 %collective-permute-start = (f32[6,512]{1,0:T(8,128)S(1)}, f32[6,512]{1,0:T(8,128)S(1)}, u32[]{:S(2)}, u32[]{:S(2)}) collective-permute-start(f32[6,512]{1,0:T(8,128)S(1)} %bitcast.11), channel_id=1, source_target_pairs={{0,1},{1,0},{2,3},{3,2},{4,5},{5,4},{6,7},{7,6},{8,9},{9,8},{10,11... | collective-permute-start | bytes 36872 | tf_op jit(solution)/shard_map/ppermute | solution.py:282
Sparse Core Ops, SparseCore 0:
  10.1 49.2 all-gather.2

commit v3 on v2

v3 whole, which is shorter than its diff:
```python
import jax
import jax.numpy as jnp
from jax import lax
from jax.experimental import pallas as pl
from jax.experimental.pallas import tpu as pltpu
from jax.sharding import Mesh
from jax.sharding import PartitionSpec as P

HD = 128
PAGE = 16
NEW = 3
SLOTS = 2
CHUNK = 512
FLOOR = -1e30
SCALE = HD ** (-0.5)
LOG2E = 1.4426950408889634
ABSENT = 1024.0

SEQ = ("z", "core")
BATCH = ("y", "x")

f32 = jnp.float32
bf16 = jnp.bfloat16
MIB = 1024 * 1024
VMEM = pl.BlockSpec(memory_space=pltpu.VMEM)
SMEM = pl.BlockSpec(memory_space=pltpu.SMEM)
ANY = pl.BlockSpec(memory_space=pl.ANY)
NT = (((1,), (1,)), ((), ()))
NN = (((1,), (0,)), ((), ()))


def dot(a, b, dims=NN):
    return lax.dot_general(a, b, dims, preferred_element_type=f32)


def exact_dot(a, b, dims=NN):
    return lax.dot_general(
        a, b, dims, precision=lax.Precision.HIGHEST, preferred_element_type=f32
    )


def split(x, terms):
    out = []
    for _ in range(terms):
        part = x.astype(bf16)
        out.append(part)
        x = x - part.astype(f32)
    return out


def down(row, count):
    return jnp.broadcast_to(row, (row.shape[1], row.shape[1])).T[:count]


def pack_kernel(owner_ref, k_ref, v_ref, send_ref, kv_ref):
    cols = k_ref.shape[1]
    pages = k_ref.shape[0] // PAGE
    send_ref[:, :, :cols] = jnp.full((send_ref.shape[0], SLOTS * PAGE, cols), ABSENT, bf16)
    send_ref[:, :, cols:] = jnp.zeros((send_ref.shape[0], SLOTS * PAGE, cols), bf16)
    kv_ref[:, :cols] = k_ref[...]
    kv_ref[:, cols:] = v_ref[...]
    owners = [owner_ref[j] for j in range(pages)]
    for j in range(pages):
        slot = jnp.int32(0)
        for i in range(j):
            slot = slot + (owners[i] == owners[j]).astype(jnp.int32)
        slot = jnp.minimum(slot, SLOTS - 1)
        rows = pl.ds(pl.multiple_of(slot * PAGE, PAGE), PAGE)
        send_ref[owners[j], rows, :cols] = k_ref[j * PAGE : (j + 1) * PAGE, :]
        send_ref[owners[j], rows, cols:] = v_ref[j * PAGE : (j + 1) * PAGE, :]


def cached_kernel(
    seq_ref, table_ref, length_ref, q_ref, ck_ref, cv_ref, dk_ref, dv_ref,
    terms_ref, state_ref, mixed_ref, q_wide, pool_k, pool_v,
):
    seq = seq_ref[0]
    heads = q_ref.shape[1] // HD
    half = heads // 2
    requests, entries = table_ref.shape
    each = requests * NEW
    rows_used = heads * each
    lanes = q_wide.shape[0]
    cols = ck_ref.shape[2]
    q_wide[...] = jnp.zeros_like(q_wide)
    for h in range(heads):
        at = (h // half) * HD
        q_wide[h * each : (h + 1) * each, at : at + HD] = q_ref[:each, h * HD : (h + 1) * HD]
    for r in range(requests):
        for j in range(entries):
            rows = slice((r * entries + j) * PAGE, (r * entries + j + 1) * PAGE)
            page = table_ref[r, j]
            pool_k[rows, :] = ck_ref[page]
            pool_v[rows, :] = cv_ref[page]
    terms = split(q_wide[...], 3)
    for i, part in enumerate(terms):
        terms_ref[i] = part
    pool_scores = sum(dot(pool_k[...], part, NT) for part in terms) * SCALE
    pool_rows = requests * entries * PAGE
    key_at = lax.broadcasted_iota(jnp.int32, (pool_rows, lanes), 0)
    lane = lax.broadcasted_iota(jnp.int32, (pool_rows, lanes), 1)
    lane_request = lane % requests
    key_request = key_at // (entries * PAGE)
    local_at = key_at % (entries * PAGE)
    position = ((local_at // PAGE) * 16 + seq) * PAGE + local_at % PAGE
    length = jnp.where(key_request == 0, length_ref[0], length_ref[1])
    pool_valid = (position < length) & (lane_request == key_request)
    new_at = lax.broadcasted_iota(jnp.int32, (8, lanes), 0)
    new_lane = lax.broadcasted_iota(jnp.int32, (8, lanes), 1) % each
    new_valid = (
        (new_at < each)
        & (new_at % requests == new_lane % requests)
        & (new_at // requests <= new_lane // requests)
        & (seq == 0)
    )
    new_scores = exact_dot(dk_ref[...], q_wide[...], NT) * SCALE
    peak = jnp.maximum(
        jnp.max(jnp.where(pool_valid, pool_scores, FLOOR), axis=0, keepdims=True),
        jnp.max(jnp.where(new_valid, new_scores, FLOOR), axis=0, keepdims=True),
    )
    pool_w = jnp.where(pool_valid, jnp.exp(pool_scores - peak), 0.0)
    new_w = jnp.where(new_valid, jnp.exp(new_scores - peak), 0.0)
    total = jnp.sum(pool_w, axis=0, keepdims=True) + jnp.sum(new_w, axis=0, keepdims=True)
    mixed = sum(dot(part, pool_v[...]) for part in split(pool_w.T, 3))
    tall_w = jnp.concatenate([new_w, jnp.zeros((lanes - 8, lanes), f32)], axis=0).T
    tall_v = jnp.concatenate([dv_ref[...], jnp.zeros((lanes - 8, cols), f32)], axis=0)
    mixed = mixed + exact_dot(tall_w, tall_v)
    mixed_ref[: half * each, :] = mixed[: half * each, :HD]
    mixed_ref[half * each : rows_used, :] = mixed[half * each : rows_used, HD:]
    state_ref[0:1, :] = peak
    state_ref[1:2, :] = total
    state_ref[2:, :] = jnp.zeros((6, lanes), f32)


def received_kernel(terms_ref, state_ref, mixed_ref, recv_ref, out_ref):
    lanes = terms_ref.shape[1]
    cols = terms_ref.shape[2]
    rows_used = mixed_ref.shape[0]
    half = rows_used // 2
    recv_rows = recv_ref.shape[0]
    keys = recv_ref[:, :cols]
    scores = sum(dot(keys, terms_ref[i], NT) for i in range(3)) * SCALE
    valid = jnp.broadcast_to(keys[:, 0:1].astype(f32) < 0.5 * ABSENT, (recv_rows, lanes))
    before = state_ref[0:1, :]
    peak = jnp.maximum(
        before, jnp.max(jnp.where(valid, scores, FLOOR), axis=0, keepdims=True)
    )
    weights = jnp.where(valid, jnp.exp(scores - peak), 0.0)
    factor = jnp.exp(before - peak)
    total = state_ref[1:2, :] * factor + jnp.sum(weights, axis=0, keepdims=True)
    mixed = sum(dot(part, recv_ref[:, cols:]) for part in split(weights.T, 3))
    kept = mixed_ref[...] * down(factor, rows_used)
    out_ref[:half, :] = kept[:half] + mixed[:half, :HD]
    out_ref[half:rows_used, :] = kept[half:] + mixed[half:rows_used, HD:]
    out_ref[rows_used : rows_used + 1, :] = peak
    out_ref[rows_used + 1 : rows_used + 2, :] = total
    out_ref[rows_used + 2 :, :] = jnp.zeros((6, lanes), f32)


def finish_kernel(all_ref, w_ref, out_ref, attention):
    count = all_ref.shape[0]
    heads = attention.shape[1] // HD
    rows_used = all_ref.shape[1] - 8
    each = rows_used // heads
    peaks = jnp.concatenate([all_ref[s, rows_used : rows_used + 1, :] for s in range(count)], axis=0)
    totals = jnp.concatenate(
        [all_ref[s, rows_used + 1 : rows_used + 2, :] for s in range(count)], axis=0
    )
    factor = jnp.exp(peaks - jnp.max(peaks, axis=0, keepdims=True))
    share = factor / jnp.sum(factor * totals, axis=0, keepdims=True)
    share = jnp.concatenate([share, jnp.zeros((HD - count, HD), f32)], axis=0).T[:rows_used]
    mixed = share[:, 0:1] * all_ref[0, :rows_used, :]
    for s in range(1, count):
        mixed = mixed + share[:, s : s + 1] * all_ref[s, :rows_used, :]
    attention[...] = jnp.zeros_like(attention)
    for h in range(heads):
        attention[:each, h * HD : (h + 1) * HD] = mixed[h * each : (h + 1) * each, :]
    w = w_ref[...]
    result = jnp.zeros((8, w.shape[1]), f32)
    for part in split(attention[...], 3):
        result = result + dot(part, w)
    pair = out_ref.shape[1]
    for n in range(out_ref.shape[0]):
        out_ref[n] = result[n * pair : (n + 1) * pair, :]


def prefill_kernel(seq_ref, q_hbm, kv_hbm, out_ref, q_ref, kv_ref, sems):
    seq = seq_ref[0]
    tokens = q_ref.shape[0]
    heads = q_ref.shape[1] // HD
    span = kv_ref.shape[0]
    group = heads // 2
    columns = [slice(i * HD, (i + 1) * HD) for i in range(4)]
    def attend(low, width):
        chunk = min(CHUNK, width - low)
        copies = [
            pltpu.make_async_copy(q_hbm, q_ref, sems.at[0]),
            pltpu.make_async_copy(kv_hbm.at[:width], kv_ref.at[:width], sems.at[1]),
        ]
        for copy in copies:
            copy.start()
        for copy in copies:
            copy.wait()
        q_at = lax.broadcasted_iota(jnp.int32, (2 * tokens, width - low), 0) % tokens + seq * tokens
        k_at = lax.broadcasted_iota(jnp.int32, (2 * tokens, width - low), 1) + low
        visible = k_at <= q_at

        def scores_of(pair):
            k = 2 * pair // group
            q = jnp.concatenate(
                [q_ref[:, h * HD : (h + 1) * HD] for h in (2 * pair, 2 * pair + 1)], axis=0
            )
            blocks = []
            for c in range(0, width, chunk):
                s = dot(q, kv_ref[c : c + chunk, columns[k]], NT)
                if c >= low:
                    s = jnp.where(visible[:, c - low : c - low + chunk], s, FLOOR)
                blocks.append(s)
            return blocks

        def finish(pair, blocks):
            k = 2 * pair // group
            peak = blocks[0]
            for s in blocks[1:]:
                peak = jnp.maximum(peak, s)
            peak = jnp.max(peak, axis=1, keepdims=True)
            mixed, total = None, None
            for i, s in enumerate(blocks):
                p = jnp.exp2((s - peak) * (SCALE * LOG2E))
                part = dot(p.astype(bf16), kv_ref[i * chunk : (i + 1) * chunk, columns[2 + k]])
                mixed = part if mixed is None else mixed + part
                total = p if total is None else total + p
            result = (mixed / jnp.sum(total, axis=1, keepdims=True)).astype(bf16)
            for n, h in enumerate((2 * pair, 2 * pair + 1)):
                out_ref[:, h * HD : (h + 1) * HD] = result[n * tokens : (n + 1) * tokens, :]

        now = scores_of(0)
        for pair in range(heads // 2):
            later = scores_of(pair + 1) if pair + 1 < heads // 2 else None
            finish(pair, now)
            now = later

    low, width = 0, 2 * tokens
    while low < span:
        inside = (seq * tokens >= low) & (seq * tokens < width)
        pl.when(inside)(lambda low=low, width=width: attend(low, width))
        low, width = width, 2 * width


def local(
    pre_q, pre_k, pre_v, owner_map, cache_k, cache_v, tables, lengths, dec_q, dec_k, dec_v, w_out
):
    seq = lax.axis_index(SEQ).astype(jnp.int32).reshape(1)
    owners = lax.axis_size(BATCH)
    swap = [(0, 1), (1, 0)]
    tokens, cols = pre_k.shape[1], pre_k.shape[2]
    requests, new, q_cols = dec_q.shape
    rows_used = q_cols // HD * requests * new
    small = pltpu.CompilerParams(vmem_limit_bytes=16 * MIB)

    def rows8(x):
        x = x.transpose(1, 0, 2).reshape(requests * new, x.shape[-1])
        return jnp.pad(x, ((0, 8 - requests * new), (0, 0)))

    send, kv = pl.pallas_call(
        pack_kernel,
        out_shape=(
            jax.ShapeDtypeStruct((owners, SLOTS * PAGE, 2 * cols), bf16),
            jax.ShapeDtypeStruct((tokens, 2 * cols), bf16),
        ),
        in_specs=[SMEM, VMEM, VMEM],
        out_specs=(VMEM, VMEM),
        name="pack_pages",
    )(owner_map.reshape(-1), pre_k[0], pre_v[0])
    received = lax.all_to_all(send, BATCH, 0, 0, tiled=True)

    all_kv = lax.all_gather(kv, SEQ, axis=0, tiled=True)
    entries = tables.shape[1]
    terms, state, mixed = pl.pallas_call(
        cached_kernel,
        out_shape=(
            jax.ShapeDtypeStruct((3, HD, 2 * HD), bf16),
            jax.ShapeDtypeStruct((8, HD), f32),
            jax.ShapeDtypeStruct((rows_used, HD), f32),
        ),
        in_specs=[SMEM, SMEM, SMEM] + [VMEM] * 5,
        out_specs=(VMEM, VMEM, VMEM),
        scratch_shapes=[
            pltpu.VMEM((HD, 2 * HD), f32),
            pltpu.VMEM((requests * entries * PAGE, cols), bf16),
            pltpu.VMEM((requests * entries * PAGE, cols), bf16),
        ],
        compiler_params=small,
        name="cached_partial",
    )(
        seq, tables, lengths, rows8(dec_q), cache_k, cache_v,
        rows8(dec_k), rows8(dec_v),
    )
    partial_state = pl.pallas_call(
        received_kernel,
        out_shape=jax.ShapeDtypeStruct((rows_used + 8, HD), f32),
        in_specs=[VMEM] * 4,
        out_specs=VMEM,
        compiler_params=small,
        name="received_partial",
    )(terms, state, mixed, received.reshape(owners * SLOTS * PAGE, 2 * cols))
    gathered = lax.all_gather(partial_state, SEQ)
    mine = pl.pallas_call(
        finish_kernel,
        out_shape=jax.ShapeDtypeStruct((new, requests, w_out.shape[1]), f32),
        in_specs=[VMEM, VMEM],
        out_specs=VMEM,
        scratch_shapes=[pltpu.VMEM((8, q_cols), f32)],
        compiler_params=small,
        name="finish_decode",
    )(gathered, w_out)
    other = lax.ppermute(mine, "tp", swap)

    group = q_cols // HD // 2
    span = all_kv.shape[0]
    pre_q, all_kv, mine = lax.optimization_barrier((pre_q, all_kv, mine))
    pre_out = pl.pallas_call(
        prefill_kernel,
        out_shape=jax.ShapeDtypeStruct((tokens, q_cols), bf16),
        in_specs=[SMEM, ANY, ANY],
        out_specs=VMEM,
        scratch_shapes=[
            pltpu.VMEM((tokens, q_cols), bf16),
            pltpu.VMEM((span, 2 * cols), bf16),
            pltpu.SemaphoreType.DMA((2,)),
        ],
        compiler_params=pltpu.CompilerParams(vmem_limit_bytes=60 * MIB),
        cost_estimate=pl.CostEstimate(
            flops=8 * group * tokens * span * HD,
            bytes_accessed=4 * MIB,
            transcendentals=2 * group * tokens * span,
        ),
        name="prefill_attention",
    )(seq, pre_q[0], all_kv)
    pre_out, other = lax.optimization_barrier((pre_out, other))
    dec_out = (mine + other).transpose(1, 0, 2)
    return (pre_out[None], dec_out)


def solution(mesh):
    cut = Mesh(mesh.devices.reshape(8, 2, 4, 4, 2), ("z", "core", "y", "x", "tp"))
    placed = (
        P(BATCH, SEQ, "tp"),
        P(BATCH, SEQ, "tp"),
        P(BATCH, SEQ, "tp"),
        P(BATCH, SEQ, None),
        P(BATCH, SEQ, "tp"),
        P(BATCH, SEQ, "tp"),
        P(BATCH, SEQ),
        P(BATCH),
        P(BATCH, None, "tp"),
        P(BATCH, None, "tp"),
        P(BATCH, None, "tp"),
        P("tp", SEQ),
    )
    return jax.shard_map(
        local,
        mesh=cut,
        in_specs=placed,
        out_specs=(P(BATCH, SEQ, "tp"), P(BATCH, None, SEQ)),
        check_vma=False,
    )
```

time: 82 us -> 78.1 us (0.952)
  waiting for transfers between devices: 10.1 us -> 5.89 us
  Pallas kernels: 7.48 us -> 8.38 us
    all_to_all x1, waiting for transfers between devices: 10.1 us -> 5.85 us  [local(): received = lax.all_to_all(send, BATCH, 0, 0, tiled=True)]
    unnamed x18 -> x10, local copies, waits for them, and re-layouts: 5.86 us -> 3.01 us
    reshape x4 -> x3, local copies, waits for them, and re-layouts: 0.06 us -> 2.24 us  [rows8(): x = x.transpose(1, 0, 2).reshape(requests * new, x.shape[-1])]
    pallas_call x2 -> x3, Pallas kernels: 2.77 us -> 3.36 us  [the longest x1 1.26 us: local(): pl.pallas_call(cached_kernel, out_shape=(jax.ShapeDtypeStruct((3, HD, 2 *...]
  transfers between devices with their start and end apart: 3 -> 3, of which waited for: 1 -> 1; matrix products, arithmetic and copies ran while one was open for 3% -> 3% of each run, Pallas kernels for 5% -> 8%
where the time goes in v3:
time: 78.1 us; the launch traced here: 77.5 us
  blocking collectives  29.9 us (38%)
  between operations  14.1 us (18%)
  starting transfers between devices  13.3 us (17%)
  Pallas kernels  8.38 us (11%)
  waiting for transfers between devices  5.89 us (8%)
  local copies, waits for them, and re-layouts  5.27 us (7%)
    all_gather x1, blocking collectives, local(): gathered = lax.all_gather(partial_state, SEQ)  29.9 us
    all_to_all x1, starting transfers between devices, local(): received = lax.all_to_all(send, BATCH, 0, 0, tiled=True)  8 us
    all_to_all x1, waiting for transfers between devices, local(): received = lax.all_to_all(send, BATCH, 0, 0, tiled=True)  5.85 us
    ppermute x1, starting transfers between devices, local(): other = lax.ppermute(mine, 'tp', swap)  5.3 us
    pallas_call x1, Pallas kernels, local(): pl.pallas_call(prefill_kernel, out_shape=jax.ShapeDtypeStruct((tokens, q_...  3.1 us
    unnamed x10, local copies, waits for them, and re-layouts  3.01 us
    reshape x3, local copies, waits for them, and re-layouts, rows8(): x = x.transpose(1, 0, 2).reshape(requests * new, x.shape[-1])  2.24 us
    pallas_call x1, Pallas kernels, local(): pl.pallas_call(pack_kernel, out_shape=(jax.ShapeDtypeStruct((owners, SLOT...  1.93 us
  transfers between devices with their start and end apart: 3, of which 1 were waited for; matrix products, arithmetic and copies ran while one was open for 3% of the time, Pallas kernels for 8%

profile of v3, /device:TPU:1, one launch (start us, length us, event | category | flops | bytes accessed | tf_op | source)
XLA Modules:
  0.0 77.5 jit_solution(15234265442525300762)
XLA Ops:
  7.2 0.0 copy-start
  7.2 0.0 all-gather.3.cloned.1.call-start
  7.2 1.9 %pack_pages.1 = (bf16[16,32,512]{2,1,0:T(8,128)(2,1)}, bf16[128,512]{1,0:T(8,128)(2,1)}) custom-call(s32[8]{0:T(128)} %bitcast.20, bf16[128,256]{1,0:T(8,128)(2,1)} %bitcast.15, bf16[128,256]{1,0:T(8,128)(2,1)} %bitcast.16), custom_call_target="tpu_custom_call" | custom-call | tf_op jit(solution)/shard_map/pack_pages/pallas_call | solution.py:265
  9.1 0.0 all-gather.3.cloned.1.call-update
  9.2 8.0 %all-to-all-start = ((bf16[16,32,512]{2,1,0:T(8,128)(2,1)}), bf16[16,32,512]{2,1,0:T(8,128)(2,1)S(1)}, u32[]{:S(2)}, u32[]{:S(2)}) async-start(bf16[16,32,512]{2,1,0:T(8,128)(2,1)} %get-tuple-element.16), calls=%async_computation | async-start | bytes 1048576 | tf_op jit(solution)/shard_map/all_to_all | solution.py:275
  17.2 0.8 %reshape.24 = f32[6,2048]{1,0:T(8,128)S(1)} reshape(f32[3,2,2048]{2,1,0:T(2,128)} %bitcast.17) | data formatting | bytes 98304 | tf_op jit(solution)/shard_map/reshape | solution.py:262
  18.0 0.7 reshape.25
  18.8 0.7 reshape.26
  19.5 0.0 copy-start.1
  19.5 0.8 %copy-done.1 = bf16[8,16,256]{2,1,0:T(8,128)(2,1)S(1)} copy-done((bf16[8,16,256]{2,1,0:T(8,128)(2,1)S(1)}, bf16[8,16,256]{2,1,0:T(8,128)(2,1)}, u32[]{:S(2)}) %copy-start.1) | copy-done | bytes 65560
  20.3 0.0 copy-start.2
  20.3 0.8 %copy-done.2 = bf16[8,16,256]{2,1,0:T(8,128)(2,1)S(1)} copy-done((bf16[8,16,256]{2,1,0:T(8,128)(2,1)S(1)}, bf16[8,16,256]{2,1,0:T(8,128)(2,1)}, u32[]{:S(2)}) %copy-start.2) | copy-done | bytes 65560
  21.2 0.0 copy-start.3
  21.2 0.7 copy-done.3
  21.8 0.0 copy-start.4
  21.8 0.7 copy-done.4
  22.5 1.3 %cached_partial.1 = (bf16[3,128,256]{2,1,0:T(8,128)(2,1)S(1)}, f32[8,128]{1,0:T(8,128)S(1)}, f32[96,128]{1,0:T(8,128)S(1)}) custom-call(s32[1]{0:T(128)} %bitcast.seq_ref, s32[2,4]{1,0:T(2,128)S(1)} %copy-done.3, s32[2]{0:T(128)S(1)} %copy-done.4, f32[8,2048]{1,0:T(8,128)S(1)} %pad.11.q_ref, bf16[8,16,256]{2,1,0:T(8,128)(2,1)S(1)} %copy-done.1, ...), custom_call_target="tpu_custom_call" | custom-call | tf_op jit(solution)/shard_map/cached_partial/pallas_call | solution.py:279
  23.8 5.9 %all-to-all-done = bf16[16,32,512]{2,1,0:T(8,128)(2,1)S(1)} async-done(((bf16[16,32,512]{2,1,0:T(8,128)(2,1)}), bf16[16,32,512]{2,1,0:T(8,128)(2,1)S(1)}, u32[]{:S(2)}, u32[]{:S(2)}) %all-to-all-start) | async-done | bytes 524320 | tf_op jit(solution)/shard_map/all_to_all | solution.py:275
  29.6 0.9 %received_partial.1 = f32[104,128]{1,0:T(8,128)S(1)} custom-call(bf16[3,128,256]{2,1,0:T(8,128)(2,1)S(1)} %get-tuple-element.13.terms_ref, f32[8,128]{1,0:T(8,128)S(1)} %get-tuple-element.14.state_ref, f32[96,128]{1,0:T(8,128)S(1)} %get-tuple-element.15.mixed_ref, bf16[512,512]{1,0:T(8,128)(2,1)S(1)} %bitcast.14), custom_call_target="tpu_custom_call" | custom-call | tf_op jit(solution)/shard_map/received_partial/pallas_call | solution.py:299
  30.5 29.9 %all-gather = f32[1664,128]{1,0:T(8,128)S(1)} all-gather(f32[104,128]{1,0:T(8,128)S(1)} %received_partial.1), channel_id=2, replica_groups=mesh['z'=8,'core'=2,'y'=4,'x'=4,'tp'=2] {'z','core'}, dimensions={0}, use_global_device_ids=true | all-gather | bytes 905216 | tf_op jit(solution)/shard_map/all_gather | solution.py:307
  60.4 0.0 copy-done
  60.4 1.2 %finish_decode.1 = f32[3,2,512]{2,1,0:T(2,128)S(1)} custom-call(f32[16,104,128]{2,1,0:T(8,128)S(1)} %bitcast.13, bf16[2048,512]{1,0:T(8,128)(2,1)S(1)} %copy-done), custom_call_target="tpu_custom_call" | custom-call | tf_op jit(solution)/shard_map/finish_decode/pallas_call | solution.py:308
  61.6 5.3 %collective-permute-start = (f32[3,2,512]{2,1,0:T(2,128)S(1)}, f32[3,2,512]{2,1,0:T(2,128)S(1)}, u32[]{:S(2)}, u32[]{:S(2)}) collective-permute-start(f32[3,2,512]{2,1,0:T(2,128)S(1)} %finish_decode.1), channel_id=1, source_target_pairs={{0,1},{1,0},{2,3},{3,2},{4,5},{5,4},{6,7},{7,6},{8,9},{9,8},{10,11... | collective-permute-start | bytes 36872 | tf_op jit(solution)/shard_map/ppermute | solution.py:317
  66.9 0.0 all-gather.3.cloned.1.call-done.kv_hbm
  66.9 3.1 %prefill_attention.1 = bf16[128,2048]{1,0:T(8,128)(2,1)} custom-call(s32[1]{0:T(128)} %bitcast.seq_ref, bf16[128,2048]{1,0:T(8,128)(2,1)} %bitcast.21, bf16[2048,512]{1,0:T(8,128)(2,1)} %all-gather.3.cloned.1.call-done.kv_hbm), custom_call_target="tpu_custom_call" | custom-call | flops 2147483648 | bytes 4194304 | tf_op jit(solution)/shard_map/prefill_attention/pallas_call | solution.py:322
  70.0 0.0 collective-permute-done
  70.1 0.6 add_bitcast_fusion
  (3 shorter events, 0.0 us)
Async XLA Ops:
  7.2 53.2 %copy-start = (bf16[2048,512]{1,0:T(8,128)(2,1)S(1)}, bf16[2048,512]{1,0:T(8,128)(2,1)}, u32[]{:S(2)}) copy-start(bf16[2048,512]{1,0:T(8,128)(2,1)} %w_ref.1) | copy-start | bytes 6291460
  7.2 59.8 %all-gather.3.cloned.1.call-start = ((), (), s32[]{:S(2)}) async-start(), calls=%async_computation.1 | async-start | bytes 2228224 | tf_op jit(solution)/shard_map/all_gather | solution.py:277
  9.2 20.4 %all-to-all-start = ((bf16[16,32,512]{2,1,0:T(8,128)(2,1)}), bf16[16,32,512]{2,1,0:T(8,128)(2,1)S(1)}, u32[]{:S(2)}, u32[]{:S(2)}) async-start(bf16[16,32,512]{2,1,0:T(8,128)(2,1)} %get-tuple-element.16), calls=%async_computation | async-start | bytes 1048576 | tf_op jit(solution)/shard_map/all_to_all | solution.py:275
  19.5 0.8 %copy-start.1 = (bf16[8,16,256]{2,1,0:T(8,128)(2,1)S(1)}, bf16[8,16,256]{2,1,0:T(8,128)(2,1)}, u32[]{:S(2)}) copy-start(bf16[8,16,256]{2,1,0:T(8,128)(2,1)} %ck_ref.1) | copy-start | bytes 196612
  20.3 0.8 %copy-start.2 = (bf16[8,16,256]{2,1,0:T(8,128)(2,1)S(1)}, bf16[8,16,256]{2,1,0:T(8,128)(2,1)}, u32[]{:S(2)}) copy-start(bf16[8,16,256]{2,1,0:T(8,128)(2,1)} %cv_ref.1) | copy-start | bytes 196612
  21.2 0.7 copy-start.3
  21.8 0.7 copy-start.4
  61.6 8.4 %collective-permute-start = (f32[3,2,512]{2,1,0:T(2,128)S(1)}, f32[3,2,512]{2,1,0:T(2,128)S(1)}, u32[]{:S(2)}, u32[]{:S(2)}) collective-permute-start(f32[3,2,512]{2,1,0:T(2,128)S(1)} %finish_decode.1), channel_id=1, source_target_pairs={{0,1},{1,0},{2,3},{3,2},{4,5},{5,4},{6,7},{7,6},{8,9},{9,8},{10,11... | collective-permute-start | bytes 36872 | tf_op jit(solution)/shard_map/ppermute | solution.py:317
Sparse Core Ops, SparseCore 0:
  10.1 49.0 all-gather.2

commit v4 on v3

--- a/solution.py
+++ b/solution.py
@@ -11,6 +11,7 @@
 NEW = 3
 SLOTS = 2
 CHUNK = 512
+TAIL = 16
 FLOOR = -1e30
 SCALE = HD ** (-0.5)
 LOG2E = 1.4426950408889634
@@ -139,7 +140,8 @@
     half = rows_used // 2
     recv_rows = recv_ref.shape[0]
     keys = recv_ref[:, :cols]
-    scores = sum(dot(keys, terms_ref[i], NT) for i in range(3)) * SCALE
+    wide = dot(keys, terms_ref[...].reshape(3 * lanes, cols), NT)
+    scores = (wide[:, :lanes] + wide[:, lanes : 2 * lanes] + wide[:, 2 * lanes :]) * SCALE
     valid = jnp.broadcast_to(keys[:, 0:1].astype(f32) < 0.5 * ABSENT, (recv_rows, lanes))
     before = state_ref[0:1, :]
     peak = jnp.maximum(
@@ -148,37 +150,37 @@
     weights = jnp.where(valid, jnp.exp(scores - peak), 0.0)
     factor = jnp.exp(before - peak)
     total = state_ref[1:2, :] * factor + jnp.sum(weights, axis=0, keepdims=True)
-    mixed = sum(dot(part, recv_ref[:, cols:]) for part in split(weights.T, 3))
+    tall = dot(jnp.concatenate(split(weights.T, 2), axis=0), recv_ref[:, cols:])
+    mixed = tall[:lanes] + tall[lanes:]
     kept = mixed_ref[...] * down(factor, rows_used)
-    out_ref[:half, :] = kept[:half] + mixed[:half, :HD]
-    out_ref[half:rows_used, :] = kept[half:] + mixed[half:rows_used, HD:]
-    out_ref[rows_used : rows_used + 1, :] = peak
-    out_ref[rows_used + 1 : rows_used + 2, :] = total
-    out_ref[rows_used + 2 :, :] = jnp.zeros((6, lanes), f32)
+    out_ref[:half, :] = (kept[:half] + mixed[:half, :HD]).astype(bf16)
+    out_ref[half:rows_used, :] = (kept[half:] + mixed[half:rows_used, HD:]).astype(bf16)
+    exact = [part.astype(f32) for part in split(peak, 3) + split(total, 3)]
+    tail = jnp.concatenate(exact + [jnp.zeros((TAIL - len(exact), lanes), f32)], axis=0)
+    out_ref[rows_used:, :] = tail.astype(bf16)
 
 
 def finish_kernel(all_ref, w_ref, out_ref, attention):
     count = all_ref.shape[0]
     heads = attention.shape[1] // HD
-    rows_used = all_ref.shape[1] - 8
+    rows_used = all_ref.shape[1] - TAIL
     each = rows_used // heads
-    peaks = jnp.concatenate([all_ref[s, rows_used : rows_used + 1, :] for s in range(count)], axis=0)
-    totals = jnp.concatenate(
-        [all_ref[s, rows_used + 1 : rows_used + 2, :] for s in range(count)], axis=0
-    )
+    tails = [all_ref[s, rows_used:, :].astype(f32) for s in range(count)]
+    peaks = jnp.concatenate([t[0:1] + t[1:2] + t[2:3] for t in tails], axis=0)
+    totals = jnp.concatenate([t[3:4] + t[4:5] + t[5:6] for t in tails], axis=0)
     factor = jnp.exp(peaks - jnp.max(peaks, axis=0, keepdims=True))
     share = factor / jnp.sum(factor * totals, axis=0, keepdims=True)
     share = jnp.concatenate([share, jnp.zeros((HD - count, HD), f32)], axis=0).T[:rows_used]
-    mixed = share[:, 0:1] * all_ref[0, :rows_used, :]
+    mixed = share[:, 0:1] * all_ref[0, :rows_used, :].astype(f32)
     for s in range(1, count):
-        mixed = mixed + share[:, s : s + 1] * all_ref[s, :rows_used, :]
+        mixed = mixed + share[:, s : s + 1] * all_ref[s, :rows_used, :].astype(f32)
     attention[...] = jnp.zeros_like(attention)
     for h in range(heads):
         attention[:each, h * HD : (h + 1) * HD] = mixed[h * each : (h + 1) * each, :]
     w = w_ref[...]
-    result = jnp.zeros((8, w.shape[1]), f32)
-    for part in split(attention[...], 3):
-        result = result + dot(part, w)
+    terms = jnp.concatenate([part.astype(f32) for part in split(attention[...], 3)], axis=0)
+    tall = dot(terms.astype(bf16), w)
+    result = tall[:8] + tall[8:16] + tall[16:]
     pair = out_ref.shape[1]
     for n in range(out_ref.shape[0]):
         out_ref[n] = result[n * pair : (n + 1) * pair, :]
@@ -244,7 +246,7 @@
     while low < span:
         inside = (seq * tokens >= low) & (seq * tokens < width)
         pl.when(inside)(lambda low=low, width=width: attend(low, width))
-        low, width = width, 2 * width
+        low, width = width, width + min(width, CHUNK)
 
 
 def local(
@@ -298,7 +300,7 @@
     )
     partial_state = pl.pallas_call(
         received_kernel,
-        out_shape=jax.ShapeDtypeStruct((rows_used + 8, HD), f32),
+        out_shape=jax.ShapeDtypeStruct((rows_used + TAIL, HD), bf16),
         in_specs=[VMEM] * 4,
         out_specs=VMEM,
         compiler_params=small,

time: 78.1 us -> 76.6 us (0.981)
  waiting for transfers between devices: 5.89 us -> 7.02 us
  starting transfers between devices: 13.3 us -> 12.2 us
    ppermute x1, starting transfers between devices: 5.3 us -> 4.12 us  [local(): other = lax.ppermute(mine, 'tp', swap)]
    ppermute x1, waiting for transfers between devices: 0.01 us -> 1.13 us  [local(): other = lax.ppermute(mine, 'tp', swap)]
  transfers between devices with their start and end apart: 3 -> 3, of which waited for: 1 -> 2; matrix products, arithmetic and copies ran while one was open for 3% -> 3% of each run, Pallas kernels for 8% -> 8%
where the time goes in v4:
time: 76.6 us; the launch traced here: 76.1 us
  blocking collectives  29.2 us (38%)
  between operations  14.1 us (18%)
  starting transfers between devices  12.2 us (16%)
  Pallas kernels  7.69 us (10%)
  waiting for transfers between devices  7.02 us (9%)
  local copies, waits for them, and re-layouts  5.27 us (7%)
    all_gather x1, blocking collectives, local(): gathered = lax.all_gather(partial_state, SEQ)  29.2 us
    all_to_all x1, starting transfers between devices, local(): received = lax.all_to_all(send, BATCH, 0, 0, tiled=True)  8 us
    all_to_all x1, waiting for transfers between devices, local(): received = lax.all_to_all(send, BATCH, 0, 0, tiled=True)  5.85 us
    ppermute x1, starting transfers between devices, local(): other = lax.ppermute(mine, 'tp', swap)  4.12 us
    pallas_call x1, Pallas kernels, local(): pl.pallas_call(prefill_kernel, out_shape=jax.ShapeDtypeStruct((tokens, q_...  3.1 us
    unnamed x10, local copies, waits for them, and re-layouts  3.01 us
    reshape x3, local copies, waits for them, and re-layouts, rows8(): x = x.transpose(1, 0, 2).reshape(requests * new, x.shape[-1])  2.24 us
    pallas_call x1, Pallas kernels, local(): pl.pallas_call(pack_kernel, out_shape=(jax.ShapeDtypeStruct((owners, SLOT...  1.93 us
  transfers between devices with their start and end apart: 3, of which 2 were waited for; matrix products, arithmetic and copies ran while one was open for 3% of the time, Pallas kernels for 8%

profile of v4, /device:TPU:1, one launch (start us, length us, event | category | flops | bytes accessed | tf_op | source)
XLA Modules:
  0.0 76.1 jit_solution(603759784682473591)
XLA Ops:
  7.2 0.0 copy-start
  7.2 0.0 all-gather.3.cloned.1.call-start
  7.2 1.9 %pack_pages.1 = (bf16[16,32,512]{2,1,0:T(8,128)(2,1)}, bf16[128,512]{1,0:T(8,128)(2,1)}) custom-call(s32[8]{0:T(128)} %bitcast.20, bf16[128,256]{1,0:T(8,128)(2,1)} %bitcast.15, bf16[128,256]{1,0:T(8,128)(2,1)} %bitcast.16), custom_call_target="tpu_custom_call" | custom-call | tf_op jit(solution)/shard_map/pack_pages/pallas_call | solution.py:267
  9.1 0.0 all-gather.3.cloned.1.call-update
  9.2 8.0 %all-to-all-start = ((bf16[16,32,512]{2,1,0:T(8,128)(2,1)}), bf16[16,32,512]{2,1,0:T(8,128)(2,1)S(1)}, u32[]{:S(2)}, u32[]{:S(2)}) async-start(bf16[16,32,512]{2,1,0:T(8,128)(2,1)} %get-tuple-element.16), calls=%async_computation | async-start | bytes 1048576 | tf_op jit(solution)/shard_map/all_to_all | solution.py:277
  17.2 0.8 %reshape.24 = f32[6,2048]{1,0:T(8,128)S(1)} reshape(f32[3,2,2048]{2,1,0:T(2,128)} %bitcast.17) | data formatting | bytes 98304 | tf_op jit(solution)/shard_map/reshape | solution.py:264
  18.0 0.7 reshape.25
  18.8 0.7 reshape.26
  19.5 0.0 copy-start.1
  19.5 0.8 %copy-done.1 = bf16[8,16,256]{2,1,0:T(8,128)(2,1)S(1)} copy-done((bf16[8,16,256]{2,1,0:T(8,128)(2,1)S(1)}, bf16[8,16,256]{2,1,0:T(8,128)(2,1)}, u32[]{:S(2)}) %copy-start.1) | copy-done | bytes 65560
  20.3 0.0 copy-start.2
  20.3 0.8 %copy-done.2 = bf16[8,16,256]{2,1,0:T(8,128)(2,1)S(1)} copy-done((bf16[8,16,256]{2,1,0:T(8,128)(2,1)S(1)}, bf16[8,16,256]{2,1,0:T(8,128)(2,1)}, u32[]{:S(2)}) %copy-start.2) | copy-done | bytes 65560
  21.2 0.0 copy-start.3
  21.2 0.7 copy-done.3
  21.8 0.0 copy-start.4
  21.8 0.7 copy-done.4
  22.5 1.3 %cached_partial.1 = (bf16[3,128,256]{2,1,0:T(8,128)(2,1)S(1)}, f32[8,128]{1,0:T(8,128)S(1)}, f32[96,128]{1,0:T(8,128)S(1)}) custom-call(s32[1]{0:T(128)} %bitcast.seq_ref, s32[2,4]{1,0:T(2,128)S(1)} %copy-done.3, s32[2]{0:T(128)S(1)} %copy-done.4, f32[8,2048]{1,0:T(8,128)S(1)} %pad.11.q_ref, bf16[8,16,256]{2,1,0:T(8,128)(2,1)S(1)} %copy-done.1, ...), custom_call_target="tpu_custom_call" | custom-call | tf_op jit(solution)/shard_map/cached_partial/pallas_call | solution.py:281
  23.8 5.9 %all-to-all-done = bf16[16,32,512]{2,1,0:T(8,128)(2,1)S(1)} async-done(((bf16[16,32,512]{2,1,0:T(8,128)(2,1)}), bf16[16,32,512]{2,1,0:T(8,128)(2,1)S(1)}, u32[]{:S(2)}, u32[]{:S(2)}) %all-to-all-start) | async-done | bytes 524320 | tf_op jit(solution)/shard_map/all_to_all | solution.py:277
  29.6 0.6 received_partial.1
  30.3 29.2 %all-gather = bf16[1792,128]{1,0:T(8,128)(2,1)S(1)} all-gather(bf16[112,128]{1,0:T(8,128)(2,1)S(1)} %received_partial.1), channel_id=2, replica_groups=mesh['z'=8,'core'=2,'y'=4,'x'=4,'tp'=2] {'z','core'}, dimensions={0}, use_global_device_ids=true | all-gather | bytes 487424 | tf_op jit(solution)/shard_map/all_gather | solution.py:309
  59.5 0.0 copy-done
  59.5 0.8 finish_decode.1
  60.2 4.1 %collective-permute-start = (f32[3,2,512]{2,1,0:T(2,128)S(1)}, f32[3,2,512]{2,1,0:T(2,128)S(1)}, u32[]{:S(2)}, u32[]{:S(2)}) collective-permute-start(f32[3,2,512]{2,1,0:T(2,128)S(1)} %finish_decode.1), channel_id=1, source_target_pairs={{0,1},{1,0},{2,3},{3,2},{4,5},{5,4},{6,7},{7,6},{8,9},{9,8},{10,11... | collective-permute-start | bytes 36872 | tf_op jit(solution)/shard_map/ppermute | solution.py:319
  64.4 0.0 all-gather.3.cloned.1.call-done.kv_hbm
  64.4 3.1 %prefill_attention.1 = bf16[128,2048]{1,0:T(8,128)(2,1)} custom-call(s32[1]{0:T(128)} %bitcast.seq_ref, bf16[128,2048]{1,0:T(8,128)(2,1)} %bitcast.21, bf16[2048,512]{1,0:T(8,128)(2,1)} %all-gather.3.cloned.1.call-done.kv_hbm), custom_call_target="tpu_custom_call" | custom-call | flops 2147483648 | bytes 4194304 | tf_op jit(solution)/shard_map/prefill_attention/pallas_call | solution.py:324
  67.5 1.1 %collective-permute-done = f32[3,2,512]{2,1,0:T(2,128)S(1)} collective-permute-done((f32[3,2,512]{2,1,0:T(2,128)S(1)}, f32[3,2,512]{2,1,0:T(2,128)S(1)}, u32[]{:S(2)}, u32[]{:S(2)}) %collective-permute-start) | collective-permute-done | bytes 12320 | tf_op jit(solution)/shard_map/ppermute | solution.py:319
  68.6 0.6 add_bitcast_fusion
  (3 shorter events, 0.0 us)
Async XLA Ops:
  7.2 52.3 %copy-start = (bf16[2048,512]{1,0:T(8,128)(2,1)S(1)}, bf16[2048,512]{1,0:T(8,128)(2,1)}, u32[]{:S(2)}) copy-start(bf16[2048,512]{1,0:T(8,128)(2,1)} %w_ref.1) | copy-start | bytes 6291460
  7.2 57.2 %all-gather.3.cloned.1.call-start = ((), (), s32[]{:S(2)}) async-start(), calls=%async_computation.1 | async-start | bytes 2228224 | tf_op jit(solution)/shard_map/all_gather | solution.py:279
  9.2 20.4 %all-to-all-start = ((bf16[16,32,512]{2,1,0:T(8,128)(2,1)}), bf16[16,32,512]{2,1,0:T(8,128)(2,1)S(1)}, u32[]{:S(2)}, u32[]{:S(2)}) async-start(bf16[16,32,512]{2,1,0:T(8,128)(2,1)} %get-tuple-element.16), calls=%async_computation | async-start | bytes 1048576 | tf_op jit(solution)/shard_map/all_to_all | solution.py:277
  19.5 0.8 %copy-start.1 = (bf16[8,16,256]{2,1,0:T(8,128)(2,1)S(1)}, bf16[8,16,256]{2,1,0:T(8,128)(2,1)}, u32[]{:S(2)}) copy-start(bf16[8,16,256]{2,1,0:T(8,128)(2,1)} %ck_ref.1) | copy-start | bytes 196612
  20.3 0.8 %copy-start.2 = (bf16[8,16,256]{2,1,0:T(8,128)(2,1)S(1)}, bf16[8,16,256]{2,1,0:T(8,128)(2,1)}, u32[]{:S(2)}) copy-start(bf16[8,16,256]{2,1,0:T(8,128)(2,1)} %cv_ref.1) | copy-start | bytes 196612
  21.2 0.7 copy-start.3
  21.8 0.7 copy-start.4
  60.2 8.4 %collective-permute-start = (f32[3,2,512]{2,1,0:T(2,128)S(1)}, f32[3,2,512]{2,1,0:T(2,128)S(1)}, u32[]{:S(2)}, u32[]{:S(2)}) collective-permute-start(f32[3,2,512]{2,1,0:T(2,128)S(1)} %finish_decode.1), channel_id=1, source_target_pairs={{0,1},{1,0},{2,3},{3,2},{4,5},{5,4},{6,7},{7,6},{8,9},{9,8},{10,11... | collective-permute-start | bytes 36872 | tf_op jit(solution)/shard_map/ppermute | solution.py:319
Sparse Core Ops, SparseCore 0:
  10.1 49.2 all-gather.2

commit v5 on v4

--- a/solution.py
+++ b/solution.py
@@ -306,7 +306,8 @@
         compiler_params=small,
         name="received_partial",
     )(terms, state, mixed, received.reshape(owners * SLOTS * PAGE, 2 * cols))
-    gathered = lax.all_gather(partial_state, SEQ)
+    copies = jnp.broadcast_to(partial_state[None], (lax.axis_size(SEQ), *partial_state.shape))
+    gathered = lax.all_to_all(copies, SEQ, 0, 0, tiled=True)
     mine = pl.pallas_call(
         finish_kernel,
         out_shape=jax.ShapeDtypeStruct((new, requests, w_out.shape[1]), f32),

time: 76.6 us -> 79.9 us (1.043)
  blocking collectives: 29.2 us -> 32.4 us
    all_to_all x0 -> x1, blocking collectives: none -> 32.4 us  [local(): gathered = lax.all_to_all(copies, SEQ, 0, 0, tiled=True)]
    all_gather x1 -> x0, blocking collectives: 29.2 us -> none  [local(): gathered = lax.all_gather(partial_state, SEQ)]
  transfers between devices with their start and end apart: 3 -> 3, of which waited for: 2 -> 2; matrix products, arithmetic and copies ran while one was open for 3% -> 3% of each run, Pallas kernels for 8% -> 7%
where the time goes in v5:
time: 79.9 us; the launch traced here: 79.4 us
  blocking collectives  32.4 us (41%)
  between operations  14.1 us (18%)
  starting transfers between devices  12.5 us (16%)
  Pallas kernels  7.69 us (10%)
  waiting for transfers between devices  6.71 us (8%)
  local copies, waits for them, and re-layouts  5.33 us (7%)
    all_to_all x1, blocking collectives, local(): gathered = lax.all_to_all(copies, SEQ, 0, 0, tiled=True)  32.4 us
    all_to_all x1, starting transfers between devices, local(): received = lax.all_to_all(send, BATCH, 0, 0, tiled=True)  8 us
    all_to_all x1, waiting for transfers between devices, local(): received = lax.all_to_all(send, BATCH, 0, 0, tiled=True)  5.85 us
    ppermute x1, starting transfers between devices, local(): other = lax.ppermute(mine, 'tp', swap)  4.46 us
    pallas_call x1, Pallas kernels, local(): pl.pallas_call(prefill_kernel, out_shape=jax.ShapeDtypeStruct((tokens, q_...  3.1 us
    unnamed x10, local copies, waits for them, and re-layouts  3.01 us
    reshape x3, local copies, waits for them, and re-layouts, rows8(): x = x.transpose(1, 0, 2).reshape(requests * new, x.shape[-1])  2.24 us
    pallas_call x1, Pallas kernels, local(): pl.pallas_call(pack_kernel, out_shape=(jax.ShapeDtypeStruct((owners, SLOT...  1.93 us
  transfers between devices with their start and end apart: 3, of which 2 were waited for; matrix products, arithmetic and copies ran while one was open for 3% of the time, Pallas kernels for 7%

profile of v5, /device:TPU:1, one launch (start us, length us, event | category | flops | bytes accessed | tf_op | source)
XLA Modules:
  0.0 79.4 jit_solution(11377886329402025354)
XLA Ops:
  7.2 0.0 copy-start
  7.2 0.0 all-gather.2.cloned.1.call-start
  7.2 1.9 %pack_pages.1 = (bf16[16,32,512]{2,1,0:T(8,128)(2,1)}, bf16[128,512]{1,0:T(8,128)(2,1)}) custom-call(s32[8]{0:T(128)} %bitcast.18, bf16[128,256]{1,0:T(8,128)(2,1)} %bitcast.13, bf16[128,256]{1,0:T(8,128)(2,1)} %bitcast.14), custom_call_target="tpu_custom_call" | custom-call | tf_op jit(solution)/shard_map/pack_pages/pallas_call | solution.py:267
  9.1 0.0 all-gather.2.cloned.1.call-update
  9.2 8.0 %all-to-all-start = ((bf16[16,32,512]{2,1,0:T(8,128)(2,1)}), bf16[16,32,512]{2,1,0:T(8,128)(2,1)S(1)}, u32[]{:S(2)}, u32[]{:S(2)}) async-start(bf16[16,32,512]{2,1,0:T(8,128)(2,1)} %get-tuple-element.16), calls=%async_computation | async-start | bytes 1048576 | tf_op jit(solution)/shard_map/all_to_all | solution.py:277
  17.2 0.8 %reshape.25 = f32[6,2048]{1,0:T(8,128)S(1)} reshape(f32[3,2,2048]{2,1,0:T(2,128)} %bitcast.15) | data formatting | bytes 98304 | tf_op jit(solution)/shard_map/reshape | solution.py:264
  18.0 0.7 reshape.26
  18.8 0.7 reshape.27
  19.5 0.0 copy-start.1
  19.5 0.8 %copy-done.1 = bf16[8,16,256]{2,1,0:T(8,128)(2,1)S(1)} copy-done((bf16[8,16,256]{2,1,0:T(8,128)(2,1)S(1)}, bf16[8,16,256]{2,1,0:T(8,128)(2,1)}, u32[]{:S(2)}) %copy-start.1) | copy-done | bytes 65560
  20.3 0.0 copy-start.2
  20.3 0.8 %copy-done.2 = bf16[8,16,256]{2,1,0:T(8,128)(2,1)S(1)} copy-done((bf16[8,16,256]{2,1,0:T(8,128)(2,1)S(1)}, bf16[8,16,256]{2,1,0:T(8,128)(2,1)}, u32[]{:S(2)}) %copy-start.2) | copy-done | bytes 65560
  21.2 0.0 copy-start.3
  21.2 0.7 copy-done.3
  21.8 0.0 copy-start.4
  21.8 0.7 copy-done.4
  22.5 1.3 %cached_partial.1 = (bf16[3,128,256]{2,1,0:T(8,128)(2,1)S(1)}, f32[8,128]{1,0:T(8,128)S(1)}, f32[96,128]{1,0:T(8,128)S(1)}) custom-call(s32[1]{0:T(128)} %bitcast.seq_ref, s32[2,4]{1,0:T(2,128)S(1)} %copy-done.3, s32[2]{0:T(128)S(1)} %copy-done.4, f32[8,2048]{1,0:T(8,128)S(1)} %pad.11.q_ref, bf16[8,16,256]{2,1,0:T(8,128)(2,1)S(1)} %copy-done.1, ...), custom_call_target="tpu_custom_call" | custom-call | tf_op jit(solution)/shard_map/cached_partial/pallas_call | solution.py:281
  23.8 5.9 %all-to-all-done = bf16[16,32,512]{2,1,0:T(8,128)(2,1)S(1)} async-done(((bf16[16,32,512]{2,1,0:T(8,128)(2,1)}), bf16[16,32,512]{2,1,0:T(8,128)(2,1)S(1)}, u32[]{:S(2)}, u32[]{:S(2)}) %all-to-all-start) | async-done | bytes 524320 | tf_op jit(solution)/shard_map/all_to_all | solution.py:277
  29.6 0.6 received_partial.1
  30.3 0.1 broadcast_in_dim.4
  30.3 32.4 %all_to_all.10.all_ref = bf16[16,112,128]{2,1,0:T(8,128)(2,1)S(1)} all-to-all(bf16[16,112,128]{2,1,0:T(8,128)(2,1)S(1)} %broadcast_in_dim.4), channel_id=1, replica_groups=mesh['z'=8,'core'=2,'y'=4,'x'=4,'tp'=2] {'z','core'}, dimensions={0} | all-to-all | bytes 917504 | tf_op jit(solution)/shard_map/all_to_all | solution.py:310
  62.8 0.0 copy-done
  62.8 0.8 finish_decode.1
  63.5 4.5 %collective-permute-start = (f32[3,2,512]{2,1,0:T(2,128)S(1)}, f32[3,2,512]{2,1,0:T(2,128)S(1)}, u32[]{:S(2)}, u32[]{:S(2)}) collective-permute-start(f32[3,2,512]{2,1,0:T(2,128)S(1)} %finish_decode.1), channel_id=1, source_target_pairs={{0,1},{1,0},{2,3},{3,2},{4,5},{5,4},{6,7},{7,6},{8,9},{9,8},{10,11... | collective-permute-start | bytes 36872 | tf_op jit(solution)/shard_map/ppermute | solution.py:320
  68.0 0.0 all-gather.2.cloned.1.call-done.kv_hbm
  68.0 3.1 %prefill_attention.1 = bf16[128,2048]{1,0:T(8,128)(2,1)} custom-call(s32[1]{0:T(128)} %bitcast.seq_ref, bf16[128,2048]{1,0:T(8,128)(2,1)} %bitcast.19, bf16[2048,512]{1,0:T(8,128)(2,1)} %all-gather.2.cloned.1.call-done.kv_hbm), custom_call_target="tpu_custom_call" | custom-call | flops 2147483648 | bytes 4194304 | tf_op jit(solution)/shard_map/prefill_attention/pallas_call | solution.py:325
  71.1 0.8 %collective-permute-done = f32[3,2,512]{2,1,0:T(2,128)S(1)} collective-permute-done((f32[3,2,512]{2,1,0:T(2,128)S(1)}, f32[3,2,512]{2,1,0:T(2,128)S(1)}, u32[]{:S(2)}, u32[]{:S(2)}) %collective-permute-start) | collective-permute-done | bytes 12320 | tf_op jit(solution)/shard_map/ppermute | solution.py:320
  71.9 0.6 add_bitcast_fusion
  (3 shorter events, 0.0 us)
Async XLA Ops:
  7.2 55.6 %copy-start = (bf16[2048,512]{1,0:T(8,128)(2,1)S(1)}, bf16[2048,512]{1,0:T(8,128)(2,1)}, u32[]{:S(2)}) copy-start(bf16[2048,512]{1,0:T(8,128)(2,1)} %w_ref.1) | copy-start | bytes 6291460
  7.2 60.8 %all-gather.2.cloned.1.call-start = ((), (), s32[]{:S(2)}) async-start(), calls=%async_computation.2 | async-start | bytes 2228224 | tf_op jit(solution)/shard_map/all_gather | solution.py:279
  9.2 20.4 %all-to-all-start = ((bf16[16,32,512]{2,1,0:T(8,128)(2,1)}), bf16[16,32,512]{2,1,0:T(8,128)(2,1)S(1)}, u32[]{:S(2)}, u32[]{:S(2)}) async-start(bf16[16,32,512]{2,1,0:T(8,128)(2,1)} %get-tuple-element.16), calls=%async_computation | async-start | bytes 1048576 | tf_op jit(solution)/shard_map/all_to_all | solution.py:277
  19.5 0.8 %copy-start.1 = (bf16[8,16,256]{2,1,0:T(8,128)(2,1)S(1)}, bf16[8,16,256]{2,1,0:T(8,128)(2,1)}, u32[]{:S(2)}) copy-start(bf16[8,16,256]{2,1,0:T(8,128)(2,1)} %ck_ref.1) | copy-start | bytes 196612
  20.3 0.8 %copy-start.2 = (bf16[8,16,256]{2,1,0:T(8,128)(2,1)S(1)}, bf16[8,16,256]{2,1,0:T(8,128)(2,1)}, u32[]{:S(2)}) copy-start(bf16[8,16,256]{2,1,0:T(8,128)(2,1)} %cv_ref.1) | copy-start | bytes 196612
  21.2 0.7 copy-start.3
  21.8 0.7 copy-start.4
  63.5 8.4 %collective-permute-start = (f32[3,2,512]{2,1,0:T(2,128)S(1)}, f32[3,2,512]{2,1,0:T(2,128)S(1)}, u32[]{:S(2)}, u32[]{:S(2)}) collective-permute-start(f32[3,2,512]{2,1,0:T(2,128)S(1)} %finish_decode.1), channel_id=1, source_target_pairs={{0,1},{1,0},{2,3},{3,2},{4,5},{5,4},{6,7},{7,6},{8,9},{9,8},{10,11... | collective-permute-start | bytes 36872 | tf_op jit(solution)/shard_map/ppermute | solution.py:320
Sparse Core Ops, SparseCore 0:
  10.1 53.6 all-gather.1

commit v6 on v4

--- a/solution.py
+++ b/solution.py
@@ -178,9 +178,9 @@
     for h in range(heads):
         attention[:each, h * HD : (h + 1) * HD] = mixed[h * each : (h + 1) * each, :]
     w = w_ref[...]
-    terms = jnp.concatenate([part.astype(f32) for part in split(attention[...], 3)], axis=0)
+    terms = jnp.concatenate([part.astype(f32) for part in split(attention[...], 2)], axis=0)
     tall = dot(terms.astype(bf16), w)
-    result = tall[:8] + tall[8:16] + tall[16:]
+    result = tall[:8] + tall[8:]
     pair = out_ref.shape[1]
     for n in range(out_ref.shape[0]):
         out_ref[n] = result[n * pair : (n + 1) * pair, :]

time: 76.6 us -> 76.5 us (level)
  transfers between devices with their start and end apart: 3 -> 3, of which waited for: 2 -> 2; matrix products, arithmetic and copies ran while one was open for 3% -> 3% of each run, Pallas kernels for 8% -> 7%
where the time goes in v6:
time: 76.5 us; the launch traced here: 76 us
  blocking collectives  29.2 us (38%)
  between operations  14.1 us (18%)
  starting transfers between devices  12.2 us (16%)
  Pallas kernels  7.62 us (10%)
  waiting for transfers between devices  7.02 us (9%)
  local copies, waits for them, and re-layouts  5.27 us (7%)
    all_gather x1, blocking collectives, local(): gathered = lax.all_gather(partial_state, SEQ)  29.2 us
    all_to_all x1, starting transfers between devices, local(): received = lax.all_to_all(send, BATCH, 0, 0, tiled=True)  8 us
    all_to_all x1, waiting for transfers between devices, local(): received = lax.all_to_all(send, BATCH, 0, 0, tiled=True)  5.85 us
    ppermute x1, starting transfers between devices, local(): other = lax.ppermute(mine, 'tp', swap)  4.12 us
    pallas_call x1, Pallas kernels, local(): pl.pallas_call(prefill_kernel, out_shape=jax.ShapeDtypeStruct((tokens, q_...  3.1 us
    unnamed x10, local copies, waits for them, and re-layouts  3.01 us
    reshape x3, local copies, waits for them, and re-layouts, rows8(): x = x.transpose(1, 0, 2).reshape(requests * new, x.shape[-1])  2.24 us
    pallas_call x1, Pallas kernels, local(): pl.pallas_call(pack_kernel, out_shape=(jax.ShapeDtypeStruct((owners, SLOT...  1.93 us
  transfers between devices with their start and end apart: 3, of which 2 were waited for; matrix products, arithmetic and copies ran while one was open for 3% of the time, Pallas kernels for 7%

profile of v6, /device:TPU:1, one launch (start us, length us, event | category | flops | bytes accessed | tf_op | source)
XLA Modules:
  0.0 76.0 jit_solution(13178073434590985729)
XLA Ops:
  7.2 0.0 copy-start
  7.2 0.0 all-gather.3.cloned.1.call-start
  7.2 1.9 %pack_pages.1 = (bf16[16,32,512]{2,1,0:T(8,128)(2,1)}, bf16[128,512]{1,0:T(8,128)(2,1)}) custom-call(s32[8]{0:T(128)} %bitcast.20, bf16[128,256]{1,0:T(8,128)(2,1)} %bitcast.15, bf16[128,256]{1,0:T(8,128)(2,1)} %bitcast.16), custom_call_target="tpu_custom_call" | custom-call | tf_op jit(solution)/shard_map/pack_pages/pallas_call | solution.py:267
  9.1 0.0 all-gather.3.cloned.1.call-update
  9.2 8.0 %all-to-all-start = ((bf16[16,32,512]{2,1,0:T(8,128)(2,1)}), bf16[16,32,512]{2,1,0:T(8,128)(2,1)S(1)}, u32[]{:S(2)}, u32[]{:S(2)}) async-start(bf16[16,32,512]{2,1,0:T(8,128)(2,1)} %get-tuple-element.16), calls=%async_computation | async-start | bytes 1048576 | tf_op jit(solution)/shard_map/all_to_all | solution.py:277
  17.2 0.8 %reshape.24 = f32[6,2048]{1,0:T(8,128)S(1)} reshape(f32[3,2,2048]{2,1,0:T(2,128)} %bitcast.17) | data formatting | bytes 98304 | tf_op jit(solution)/shard_map/reshape | solution.py:264
  18.0 0.7 reshape.25
  18.8 0.7 reshape.26
  19.5 0.0 copy-start.1
  19.5 0.8 %copy-done.1 = bf16[8,16,256]{2,1,0:T(8,128)(2,1)S(1)} copy-done((bf16[8,16,256]{2,1,0:T(8,128)(2,1)S(1)}, bf16[8,16,256]{2,1,0:T(8,128)(2,1)}, u32[]{:S(2)}) %copy-start.1) | copy-done | bytes 65560
  20.3 0.0 copy-start.2
  20.3 0.8 %copy-done.2 = bf16[8,16,256]{2,1,0:T(8,128)(2,1)S(1)} copy-done((bf16[8,16,256]{2,1,0:T(8,128)(2,1)S(1)}, bf16[8,16,256]{2,1,0:T(8,128)(2,1)}, u32[]{:S(2)}) %copy-start.2) | copy-done | bytes 65560
  21.2 0.0 copy-start.3
  21.2 0.7 copy-done.3
  21.8 0.0 copy-start.4
  21.8 0.7 copy-done.4
  22.5 1.3 %cached_partial.1 = (bf16[3,128,256]{2,1,0:T(8,128)(2,1)S(1)}, f32[8,128]{1,0:T(8,128)S(1)}, f32[96,128]{1,0:T(8,128)S(1)}) custom-call(s32[1]{0:T(128)} %bitcast.seq_ref, s32[2,4]{1,0:T(2,128)S(1)} %copy-done.3, s32[2]{0:T(128)S(1)} %copy-done.4, f32[8,2048]{1,0:T(8,128)S(1)} %pad.11.q_ref, bf16[8,16,256]{2,1,0:T(8,128)(2,1)S(1)} %copy-done.1, ...), custom_call_target="tpu_custom_call" | custom-call | tf_op jit(solution)/shard_map/cached_partial/pallas_call | solution.py:281
  23.8 5.9 %all-to-all-done = bf16[16,32,512]{2,1,0:T(8,128)(2,1)S(1)} async-done(((bf16[16,32,512]{2,1,0:T(8,128)(2,1)}), bf16[16,32,512]{2,1,0:T(8,128)(2,1)S(1)}, u32[]{:S(2)}, u32[]{:S(2)}) %all-to-all-start) | async-done | bytes 524320 | tf_op jit(solution)/shard_map/all_to_all | solution.py:277
  29.6 0.6 received_partial.1
  30.3 29.2 %all-gather = bf16[1792,128]{1,0:T(8,128)(2,1)S(1)} all-gather(bf16[112,128]{1,0:T(8,128)(2,1)S(1)} %received_partial.1), channel_id=2, replica_groups=mesh['z'=8,'core'=2,'y'=4,'x'=4,'tp'=2] {'z','core'}, dimensions={0}, use_global_device_ids=true | all-gather | bytes 487424 | tf_op jit(solution)/shard_map/all_gather | solution.py:309
  59.5 0.0 copy-done
  59.5 0.7 finish_decode.1
  60.1 4.1 %collective-permute-start = (f32[3,2,512]{2,1,0:T(2,128)S(1)}, f32[3,2,512]{2,1,0:T(2,128)S(1)}, u32[]{:S(2)}, u32[]{:S(2)}) collective-permute-start(f32[3,2,512]{2,1,0:T(2,128)S(1)} %finish_decode.1), channel_id=1, source_target_pairs={{0,1},{1,0},{2,3},{3,2},{4,5},{5,4},{6,7},{7,6},{8,9},{9,8},{10,11... | collective-permute-start | bytes 36872 | tf_op jit(solution)/shard_map/ppermute | solution.py:319
  64.3 0.0 all-gather.3.cloned.1.call-done.kv_hbm
  64.3 3.1 %prefill_attention.1 = bf16[128,2048]{1,0:T(8,128)(2,1)} custom-call(s32[1]{0:T(128)} %bitcast.seq_ref, bf16[128,2048]{1,0:T(8,128)(2,1)} %bitcast.21, bf16[2048,512]{1,0:T(8,128)(2,1)} %all-gather.3.cloned.1.call-done.kv_hbm), custom_call_target="tpu_custom_call" | custom-call | flops 2147483648 | bytes 4194304 | tf_op jit(solution)/shard_map/prefill_attention/pallas_call | solution.py:324
  67.4 1.1 %collective-permute-done = f32[3,2,512]{2,1,0:T(2,128)S(1)} collective-permute-done((f32[3,2,512]{2,1,0:T(2,128)S(1)}, f32[3,2,512]{2,1,0:T(2,128)S(1)}, u32[]{:S(2)}, u32[]{:S(2)}) %collective-permute-start) | collective-permute-done | bytes 12320 | tf_op jit(solution)/shard_map/ppermute | solution.py:319
  68.5 0.6 add_bitcast_fusion
  (3 shorter events, 0.0 us)
Async XLA Ops:
  7.2 52.3 %copy-start = (bf16[2048,512]{1,0:T(8,128)(2,1)S(1)}, bf16[2048,512]{1,0:T(8,128)(2,1)}, u32[]{:S(2)}) copy-start(bf16[2048,512]{1,0:T(8,128)(2,1)} %w_ref.1) | copy-start | bytes 6291460
  7.2 57.1 %all-gather.3.cloned.1.call-start = ((), (), s32[]{:S(2)}) async-start(), calls=%async_computation.1 | async-start | bytes 2228224 | tf_op jit(solution)/shard_map/all_gather | solution.py:279
  9.2 20.4 %all-to-all-start = ((bf16[16,32,512]{2,1,0:T(8,128)(2,1)}), bf16[16,32,512]{2,1,0:T(8,128)(2,1)S(1)}, u32[]{:S(2)}, u32[]{:S(2)}) async-start(bf16[16,32,512]{2,1,0:T(8,128)(2,1)} %get-tuple-element.16), calls=%async_computation | async-start | bytes 1048576 | tf_op jit(solution)/shard_map/all_to_all | solution.py:277
  19.5 0.8 %copy-start.1 = (bf16[8,16,256]{2,1,0:T(8,128)(2,1)S(1)}, bf16[8,16,256]{2,1,0:T(8,128)(2,1)}, u32[]{:S(2)}) copy-start(bf16[8,16,256]{2,1,0:T(8,128)(2,1)} %ck_ref.1) | copy-start | bytes 196612
  20.3 0.8 %copy-start.2 = (bf16[8,16,256]{2,1,0:T(8,128)(2,1)S(1)}, bf16[8,16,256]{2,1,0:T(8,128)(2,1)}, u32[]{:S(2)}) copy-start(bf16[8,16,256]{2,1,0:T(8,128)(2,1)} %cv_ref.1) | copy-start | bytes 196612
  21.2 0.7 copy-start.3
  21.8 0.7 copy-start.4
  60.1 8.4 %collective-permute-start = (f32[3,2,512]{2,1,0:T(2,128)S(1)}, f32[3,2,512]{2,1,0:T(2,128)S(1)}, u32[]{:S(2)}, u32[]{:S(2)}) collective-permute-start(f32[3,2,512]{2,1,0:T(2,128)S(1)} %finish_decode.1), channel_id=1, source_target_pairs={{0,1},{1,0},{2,3},{3,2},{4,5},{5,4},{6,7},{7,6},{8,9},{9,8},{10,11... | collective-permute-start | bytes 36872 | tf_op jit(solution)/shard_map/ppermute | solution.py:319
Sparse Core Ops, SparseCore 0:
  10.1 49.2 all-gather.2
